TPU v7x, 32 devices: a whole 2x2x4 slice. The times are simulated.
32 devices in a mesh: dp: 8 (over z, y), tensor: 4 (over x, core).
Axes of the slice: x: 2, y: 2, z: 4, core: 2. Of those that a mesh axis runs over, the one named last changes fastest.
Arguments:
- layer_input: bfloat16 [2048, 8, 1536], P('tensor', 'dp'), may hold values from -6 to 6
- cotangent: bfloat16 [2048, 8, 1536], P('tensor', 'dp'), may hold values from -6 to 6
- lengths: int32 [8], P('dp'), may hold values from 1024 to 2048, as said below
- owners: int32 [8], replicated, may hold values from 0 to 7, each once
- weight: float32 [1536, 4, 6208], P('dp', 'tensor')
- weight_first: float32 [1536, 4, 6208], P('dp', 'tensor')
- weight_second: float32 [1536, 4, 6208], P('dp', 'tensor'), as said below
- left_basis: float32 [1536, 4, 192], P('dp', 'tensor'), as said below
- right_basis: float32 [8, 4, 97, 64, 64], P('dp', 'tensor'), as said below
- left_stat: float32 [1536, 4, 192], P('dp', 'tensor'), as said below
- right_stat: float32 [8, 4, 97, 64, 64], P('dp', 'tensor'), as said below
- norm_gains: float32 [3200], replicated
- gain_first: float32 [3200], replicated
- gain_second: float32 [3200], replicated, as said below
Outputs:
- layer_output: bfloat16 [2048, 8, 1536], P('tensor', 'dp')
- input_grad: float32 [2048, 8, 1536], P('tensor', 'dp')
- new_weight: float32 [1536, 4, 6208], P('dp', 'tensor')
- new_first: float32 [1536, 4, 6208], P('dp', 'tensor')
- new_second: float32 [1536, 4, 6208], P('dp', 'tensor')
- basis_left: float32 [1536, 4, 192], P('dp', 'tensor')
- basis_right: float32 [8, 4, 97, 64, 64], P('dp', 'tensor')
- stats_left: float32 [1536, 4, 192], P('dp', 'tensor')
- stats_right: float32 [8, 4, 97, 64, 64], P('dp', 'tensor')
- gain_moment: float32 [3200], replicated
- gain_square: float32 [3200], replicated
- new_gains: float32 [3200], replicated
Inputs may be any that keep to these rules, and one draw needn't show every extreme that they name: `lengths`: every slot holds 1024 live tokens or more; in every draw some slot is full. `owners`: each number once. `left_basis`: each 192 x 192 block of one row block and tensor index is orthogonal. `right_basis`: each 64 x 64 block is orthogonal. `left_stat`: each 192 x 192 block is symmetric with a dominant positive diagonal. `right_stat`: each 64 x 64 block is symmetric with a dominant positive diagonal. `weight_second`: positive. `gain_second`: positive.
All inputs are finite; a program needn't handle non-finite values.
Results may differ from a plain program's by a relative error of at most 0.012.
The roundings to bfloat16 on the way count: a program that leaves them out, or rounds other values in their place, can miss the bound.
Values may be sent and summed in bfloat16 or wider, within the bound.
A program may use at most 448 MiB of HBM per device.

v0:
```python
import jax
import jax.numpy as jnp
from jax import lax
from jax.sharding import PartitionSpec as P

MODEL_DIM = 1536
QUERY_HEADS = 24
KEY_VALUE_HEADS = 8
HEAD_DIM = 64
FF = 6912
QUERY_BLOCK = 512
STEP = 10


NORM_EPS = 1e-06
ROPE_THETA = 1000000.0
MOMENT_DECAY = 0.5
ADAM_EPSILON = 1e-08
RATE_WEIGHT = 0.05
RATE_GAIN = 0.3
DECAY_WEIGHT = 0.01
MASKED_SCORE = -1e30
PRECISE = lax.Precision.HIGHEST


def rms_rows(values, gain_vec):
    inverse = lax.rsqrt(jnp.mean(values * values, axis=-1, keepdims=True) + NORM_EPS)
    scaled = values * inverse
    return (scaled * gain_vec, scaled, inverse)


def norm_back(grad_norm, scaled, inverse, gain_vec):
    grad_scaled = grad_norm * gain_vec
    row_inner = jnp.mean(grad_scaled * scaled, axis=-1, keepdims=True)
    return inverse * (grad_scaled - scaled * row_inner)


def rope_tables(positions_count):
    half_dim = HEAD_DIM // 2
    frequency = ROPE_THETA ** (-(jnp.arange(half_dim, dtype=jnp.float32) * 2.0 / HEAD_DIM))
    angles = jnp.arange(positions_count, dtype=jnp.float32)[:, None] * frequency[None, :]
    return (jnp.cos(angles), jnp.sin(angles))


def table_rows(cosine, sine, values):
    half_dim = values.shape[-1] // 2
    table_shape = (cosine.shape[0],) + (1,) * (values.ndim - 2) + (half_dim,)
    return (cosine.reshape(table_shape), sine.reshape(table_shape), half_dim)


def rotate(values, cosine, sine):
    cos_rows, sin_rows, half_dim = table_rows(cosine, sine, values)
    lower_half = values[..., :half_dim]
    upper_half = values[..., half_dim:]
    return jnp.concatenate(
        [
            lower_half * cos_rows - upper_half * sin_rows,
            upper_half * cos_rows + lower_half * sin_rows,
        ],
        axis=-1,
    )


def unrotate(grads, cosine, sine):
    cos_rows, sin_rows, half_dim = table_rows(cosine, sine, grads)
    lower_half = grads[..., :half_dim]
    upper_half = grads[..., half_dim:]
    return jnp.concatenate(
        [
            lower_half * cos_rows + upper_half * sin_rows,
            upper_half * cos_rows - lower_half * sin_rows,
        ],
        axis=-1,
    )


def block_scores(query_block, key_matrix, offset, slot_length):
    scores = jnp.einsum(
        "qhgd,khd->hgqk", query_block, key_matrix, preferred_element_type=jnp.float32
    ) * HEAD_DIM ** (-0.5)
    query_pos = offset + jnp.arange(query_block.shape[0], dtype=jnp.int32)
    key_pos = jnp.arange(key_matrix.shape[0], dtype=jnp.int32)
    allowed = (key_pos[None, :] <= query_pos[:, None]) & (key_pos[None, :] < slot_length)
    return jnp.where(allowed, scores, MASKED_SCORE)


def attend_block(query_block, key_matrix, value_matrix, offset, slot_length):
    scores = block_scores(query_block, key_matrix, offset, slot_length)
    row_top = jnp.max(scores, axis=-1, keepdims=True)
    exponent = jnp.exp(scores - row_top)
    row_total = jnp.sum(exponent, axis=-1, keepdims=True)
    attn_prob = (exponent / row_total).astype(jnp.bfloat16)
    attended_output = jnp.einsum(
        "hgqk,khd->qhgd", attn_prob, value_matrix, preferred_element_type=jnp.float32
    )
    return (attended_output, (row_top + jnp.log(row_total))[..., 0])


def attend_back(query_block, key_matrix, value_matrix, grad_block, lse_block, offset, slot_length):
    scores = block_scores(query_block, key_matrix, offset, slot_length)
    attn_prob = jnp.exp(scores - lse_block[..., None])
    grad_prob = jnp.einsum(
        "qhgd,khd->hgqk", grad_block, value_matrix, preferred_element_type=jnp.float32
    )
    grad_value = jnp.einsum(
        "hgqk,qhgd->khd",
        attn_prob.astype(jnp.bfloat16),
        grad_block,
        preferred_element_type=jnp.float32,
    )
    row_inner = jnp.sum(attn_prob * grad_prob, axis=-1, keepdims=True)
    grad_score = (attn_prob * (grad_prob - row_inner)).astype(jnp.bfloat16)
    grad_query = jnp.einsum(
        "hgqk,khd->qhgd", grad_score, key_matrix, preferred_element_type=jnp.float32
    ) * HEAD_DIM ** (-0.5)
    grad_key = jnp.einsum(
        "hgqk,qhgd->khd", grad_score, query_block, preferred_element_type=jnp.float32
    ) * HEAD_DIM ** (-0.5)
    return (grad_query, grad_key, grad_value)


def gather_rows(values):
    return lax.all_gather(values, "tensor", axis=0, tiled=True)


def gather_back(values):
    return lax.all_gather(values, "tensor", axis=0, tiled=True)


def branch_sum(left_rows, right_w):
    return lax.psum_scatter(
        jnp.einsum("tsc,dc->tsd", left_rows, right_w, preferred_element_type=jnp.float32),
        "tensor",
        scatter_dimension=0,
        tiled=True,
    )


def input_sum(left_rows, right_w):
    return lax.psum_scatter(
        jnp.einsum("tsc,dc->tsd", left_rows, right_w, preferred_element_type=jnp.float32),
        "tensor",
        scatter_dimension=0,
        tiled=True,
    )


def orthonormal(matrix):
    gram_matrix = jnp.einsum("...ik,...il->...kl", matrix, matrix, precision=PRECISE)
    factor = jnp.linalg.cholesky(gram_matrix)
    return lax.linalg.triangular_solve(
        factor, matrix, left_side=False, lower=True, transpose_a=True
    )


def precondition(grad_w, weight_w, first_w, second_w, left_w, right_w, left_cov, right_cov):
    shards, own_rows, tensor_parts, cols_all = grad_w.shape
    tile_count = right_w.shape[2]
    tile_width = right_w.shape[3]
    tiled = grad_w.reshape(shards, own_rows, tensor_parts, tile_count, tile_width)
    half_turn = jnp.einsum("sitj,sitbc->sjtbc", left_w, tiled, precision=PRECISE)
    turned = jnp.einsum("sjtbc,stbce->sjtbe", half_turn, right_w, precision=PRECISE).reshape(
        grad_w.shape
    )
    first_new = MOMENT_DECAY * first_w + (1.0 - MOMENT_DECAY) * turned
    second_new = MOMENT_DECAY * second_w + (1.0 - MOMENT_DECAY) * turned * turned
    correction = 1.0 - MOMENT_DECAY**STEP
    direction = first_new / correction / (jnp.sqrt(second_new / correction) + ADAM_EPSILON)
    back_half = jnp.einsum(
        "sitj,sjtbe->sitbe", left_w, direction.reshape(tiled.shape), precision=PRECISE
    )
    update = jnp.einsum("sitbe,stbce->sitbc", back_half, right_w, precision=PRECISE).reshape(
        grad_w.shape
    )
    weight_new = weight_w - RATE_WEIGHT * (update + DECAY_WEIGHT * weight_w)
    left_cov_new = MOMENT_DECAY * left_cov + (1.0 - MOMENT_DECAY) * jnp.einsum(
        "sitbc,sjtbc->sitj", tiled, tiled, precision=PRECISE
    )
    right_cov_new = MOMENT_DECAY * right_cov + (1.0 - MOMENT_DECAY) * jnp.einsum(
        "sitbc,sitbe->stbce", tiled, tiled, precision=PRECISE
    )
    left_new = orthonormal(
        jnp.einsum("sitj,sjtk->stik", left_cov_new, left_w, precision=PRECISE)
    ).transpose(0, 2, 1, 3)
    right_new = orthonormal(
        jnp.einsum("stbce,stbef->stbcf", right_cov_new, right_w, precision=PRECISE)
    )
    return (weight_new, first_new, second_new, left_new, right_new, left_cov_new, right_cov_new)


def body(
    layer_input,
    cotangent,
    lengths,
    owners,
    weight,
    weight_first,
    weight_second,
    left_basis,
    right_basis,
    left_stat,
    right_stat,
    norm_gains,
    gain_first,
    gain_second,
):
    tensor_total = lax.axis_size("tensor")
    shard_count = lax.axis_size("dp")
    rows_here, slots_here, model_width = layer_input.shape
    seq_all = rows_here * tensor_total
    own_rows = weight.shape[0]
    cols_all = weight.shape[2]
    query_cols = QUERY_HEADS * HEAD_DIM // tensor_total
    key_value_columns = KEY_VALUE_HEADS * HEAD_DIM // tensor_total
    ff_cols = FF // tensor_total
    heads_query = QUERY_HEADS // tensor_total
    key_value_heads = KEY_VALUE_HEADS // tensor_total
    group_width = QUERY_HEADS // KEY_VALUE_HEADS
    off_gate = query_cols + 2 * key_value_columns
    off_out = off_gate + 2 * ff_cols
    off_down = off_out + query_cols
    block_total = seq_all // QUERY_BLOCK
    slot_ids = jnp.arange(shard_count, dtype=jnp.int32)
    holder_of = jnp.sum(
        jnp.where(owners[None, :] == slot_ids[:, None], slot_ids[None, :], 0), axis=1
    )

    def arrange(gathered):
        block_list = gathered.reshape(shard_count, own_rows, cols_all)
        return jnp.take(block_list, owners, axis=0).reshape(shard_count * own_rows, cols_all)

    weight_low = weight.astype(jnp.bfloat16)
    joined_w = arrange(lax.all_gather(weight_low, "dp", axis=0, tiled=True))
    gain_in = norm_gains[:MODEL_DIM]
    gain_mid = norm_gains[MODEL_DIM : 2 * MODEL_DIM]
    gain_query = norm_gains[2 * MODEL_DIM : 2 * MODEL_DIM + HEAD_DIM]
    gain_key = norm_gains[2 * MODEL_DIM + HEAD_DIM :]
    cosine, sine = rope_tables(seq_all)
    input_f32 = layer_input.astype(jnp.float32)
    normalized_input, scaled_in, inverse_in = rms_rows(input_f32, gain_in)
    low_in = gather_rows(normalized_input.astype(jnp.bfloat16))
    projected = jnp.einsum(
        "tsd,dc->tsc", low_in, joined_w[:, :off_gate], preferred_element_type=jnp.float32
    )
    query_raw = projected[..., :query_cols].reshape(seq_all, slots_here, heads_query, HEAD_DIM)
    key_raw = projected[..., query_cols : query_cols + key_value_columns].reshape(
        seq_all, slots_here, key_value_heads, HEAD_DIM
    )
    value_low = (
        projected[..., query_cols + key_value_columns :]
        .astype(jnp.bfloat16)
        .reshape(seq_all, slots_here, key_value_heads, HEAD_DIM)
    )
    query_norm, query_scaled, query_inv = rms_rows(query_raw, gain_query)
    key_norm, key_scaled, key_inv = rms_rows(key_raw, gain_key)
    query_low = rotate(query_norm, cosine, sine).astype(jnp.bfloat16)
    key_low = rotate(key_norm, cosine, sine).astype(jnp.bfloat16)
    query_slots = jnp.moveaxis(query_low, 1, 0).reshape(
        slots_here, seq_all, key_value_heads, group_width, HEAD_DIM
    )
    key_slots = jnp.moveaxis(key_low, 1, 0)
    value_slots = jnp.moveaxis(value_low, 1, 0)

    def forward_slot(slot_items):
        query_one, key_one, value_one, slot_length = slot_items
        attended_parts = []
        lse_parts = []
        for block_index in range(block_total):
            offset = block_index * QUERY_BLOCK
            attended_output, lse_block = attend_block(
                query_one[offset : offset + QUERY_BLOCK], key_one, value_one, offset, slot_length
            )
            attended_parts.append(attended_output)
            lse_parts.append(lse_block)
        return (jnp.concatenate(attended_parts, axis=0), jnp.stack(lse_parts, axis=0))

    attn_slots, lse_slots = lax.map(forward_slot, (query_slots, key_slots, value_slots, lengths))
    attn_low = (
        jnp.moveaxis(attn_slots, 0, 1).reshape(seq_all, slots_here, query_cols).astype(jnp.bfloat16)
    )
    attn_sum = branch_sum(attn_low, joined_w[:, off_out:off_down])
    resid_mid = input_f32 + attn_sum
    normed_mid, scaled_mid, inverse_mid = rms_rows(resid_mid, gain_mid)
    low_mid = gather_rows(normed_mid.astype(jnp.bfloat16))
    gate_up = jnp.einsum(
        "tsd,dc->tsc", low_mid, joined_w[:, off_gate:off_out], preferred_element_type=jnp.float32
    )
    gate_val = gate_up[..., :ff_cols]
    up_val = gate_up[..., ff_cols:]
    sigmoid_gate = jax.nn.sigmoid(gate_val)
    silu_gate = gate_val * sigmoid_gate
    hidden_low = (silu_gate * up_val).astype(jnp.bfloat16)
    ffn_sum = branch_sum(hidden_low, joined_w[:, off_down:])
    layer_output = (resid_mid + ffn_sum).astype(jnp.bfloat16)
    back_w = arrange(lax.all_gather(weight_low, "dp", axis=0, tiled=True))
    tensor_pos = lax.axis_index("tensor")
    positions = tensor_pos * rows_here + jnp.arange(rows_here, dtype=jnp.int32)
    live = (positions[:, None] < lengths[None, :]).astype(jnp.float32)[..., None]
    grad_out = cotangent.astype(jnp.float32) * live
    grad_out_all = gather_back(grad_out.astype(jnp.bfloat16))
    grad_hidden = jnp.einsum(
        "tsd,dc->tsc", grad_out_all, back_w[:, off_down:], preferred_element_type=jnp.float32
    )
    grad_down_w = jnp.einsum(
        "tsd,tsc->dc", grad_out_all, hidden_low, preferred_element_type=jnp.float32
    )
    grad_up = grad_hidden * silu_gate
    grad_gate = grad_hidden * up_val * sigmoid_gate * (1.0 + gate_val * (1.0 - sigmoid_gate))
    grad_gu_low = jnp.concatenate([grad_gate, grad_up], axis=-1).astype(jnp.bfloat16)
    grad_gate_up_w = jnp.einsum(
        "tsd,tsc->dc", low_mid, grad_gu_low, preferred_element_type=jnp.float32
    )
    grad_mid_norm = input_sum(grad_gu_low, back_w[:, off_gate:off_out])
    gain_mid_grad = jnp.sum(grad_mid_norm * scaled_mid, axis=(0, 1))
    grad_resid = grad_out + norm_back(grad_mid_norm, scaled_mid, inverse_mid, gain_mid)
    grad_resid_all = gather_back(grad_resid.astype(jnp.bfloat16))
    grad_out_w = jnp.einsum(
        "tsd,tsc->dc", grad_resid_all, attn_low, preferred_element_type=jnp.float32
    )
    grad_attn = jnp.einsum(
        "tsd,dc->tsc",
        grad_resid_all,
        back_w[:, off_out:off_down],
        preferred_element_type=jnp.float32,
    ).astype(jnp.bfloat16)
    grad_attn_slots = jnp.moveaxis(
        grad_attn.reshape(seq_all, slots_here, key_value_heads, group_width, HEAD_DIM), 1, 0
    )

    def backward_slot(slot_items):
        query_one, key_one, value_one, grad_one, lse_one, slot_length = slot_items
        grad_keys = jnp.zeros(key_one.shape, jnp.float32)
        grad_values = jnp.zeros(value_one.shape, jnp.float32)
        query_parts = []
        for block_index in range(block_total):
            offset = block_index * QUERY_BLOCK
            grad_query, grad_key, grad_value = attend_back(
                query_one[offset : offset + QUERY_BLOCK],
                key_one,
                value_one,
                grad_one[offset : offset + QUERY_BLOCK],
                lse_one[block_index],
                offset,
                slot_length,
            )
            query_parts.append(grad_query)
            grad_keys = grad_keys + grad_key
            grad_values = grad_values + grad_value
        return (jnp.concatenate(query_parts, axis=0), grad_keys, grad_values)

    grad_q_slots, grad_k_slots, grad_v_slots = lax.map(
        backward_slot, (query_slots, key_slots, value_slots, grad_attn_slots, lse_slots, lengths)
    )
    grad_q_rot = jnp.moveaxis(grad_q_slots, 0, 1).reshape(
        seq_all, slots_here, heads_query, HEAD_DIM
    )
    grad_k_rot = jnp.moveaxis(grad_k_slots, 0, 1)
    grad_v_all = jnp.moveaxis(grad_v_slots, 0, 1)
    grad_q_norm = unrotate(grad_q_rot, cosine, sine)
    grad_k_norm = unrotate(grad_k_rot, cosine, sine)
    gain_query_grad = jnp.sum(grad_q_norm * query_scaled, axis=(0, 1, 2))
    gain_key_grad = jnp.sum(grad_k_norm * key_scaled, axis=(0, 1, 2))
    grad_q_raw = norm_back(grad_q_norm, query_scaled, query_inv, gain_query)
    grad_k_raw = norm_back(grad_k_norm, key_scaled, key_inv, gain_key)
    grad_qkv_low = jnp.concatenate(
        [
            grad_q_raw.reshape(seq_all, slots_here, query_cols),
            grad_k_raw.reshape(seq_all, slots_here, key_value_columns),
            grad_v_all.reshape(seq_all, slots_here, key_value_columns),
        ],
        axis=-1,
    ).astype(jnp.bfloat16)
    grad_qkv_w = jnp.einsum("tsd,tsc->dc", low_in, grad_qkv_low, preferred_element_type=jnp.float32)
    grad_in_norm = input_sum(grad_qkv_low, back_w[:, :off_gate])
    gain_in_grad = jnp.sum(grad_in_norm * scaled_in, axis=(0, 1))
    input_grad = grad_resid + norm_back(grad_in_norm, scaled_in, inverse_in, gain_in)
    gain_grad = lax.psum(
        jnp.concatenate([gain_in_grad, gain_mid_grad, gain_query_grad, gain_key_grad]),
        ("dp", "tensor"),
    )
    full_grad = jnp.concatenate([grad_qkv_w, grad_gate_up_w, grad_out_w, grad_down_w], axis=1)
    block_list = full_grad.reshape(shard_count, own_rows, full_grad.shape[1])
    reduced = lax.psum_scatter(
        jnp.take(block_list, holder_of, axis=0).reshape(
            shard_count * own_rows, 1, full_grad.shape[1]
        ),
        "dp",
        scatter_dimension=0,
        tiled=True,
    )
    block_shape = (1, own_rows, 1, cols_all)
    results = precondition(
        reduced.reshape(block_shape),
        weight.reshape(block_shape),
        weight_first.reshape(block_shape),
        weight_second.reshape(block_shape),
        left_basis.reshape(1, own_rows, 1, own_rows),
        right_basis,
        left_stat.reshape(1, own_rows, 1, own_rows),
        right_stat,
    )
    weight_new, first_new, second_new, left_new, right_new, left_cov_new, right_cov_new = results
    moment_one = MOMENT_DECAY * gain_first + (1.0 - MOMENT_DECAY) * gain_grad
    moment_two = MOMENT_DECAY * gain_second + (1.0 - MOMENT_DECAY) * gain_grad * gain_grad
    correction = 1.0 - MOMENT_DECAY**STEP
    gains_new = norm_gains - RATE_GAIN * (moment_one / correction) / (
        jnp.sqrt(moment_two / correction) + ADAM_EPSILON
    )
    return (
        layer_output,
        input_grad,
        weight_new.reshape(weight.shape),
        first_new.reshape(weight.shape),
        second_new.reshape(weight.shape),
        left_new.reshape(left_basis.shape),
        right_new,
        left_cov_new.reshape(left_stat.shape),
        right_cov_new,
        moment_one,
        moment_two,
        gains_new,
    )


def solution(mesh):
    in_specs = (
        P("tensor", "dp", None),
        P("tensor", "dp", None),
        P("dp"),
        P(),
        P("dp", "tensor", None),
        P("dp", "tensor", None),
        P("dp", "tensor", None),
        P("dp", "tensor", None),
        P("dp", "tensor", None, None, None),
        P("dp", "tensor", None),
        P("dp", "tensor", None, None, None),
        P(),
        P(),
        P(),
    )
    out_specs = (
        P("tensor", "dp", None),
        P("tensor", "dp", None),
        P("dp", "tensor", None),
        P("dp", "tensor", None),
        P("dp", "tensor", None),
        P("dp", "tensor", None),
        P("dp", "tensor", None, None, None),
        P("dp", "tensor", None),
        P("dp", "tensor", None, None, None),
        P(),
        P(),
        P(),
    )
    return jax.shard_map(body, mesh=mesh, in_specs=in_specs, out_specs=out_specs, check_vma=False)
```

profile of v0, /device:TPU:0, one launch (start us, length us, event | category | flops | bytes accessed | tf_op | source)
XLA Modules:
  0.0 3622.7 jit_solution(13875663956028271592)
XLA Ops:
  22.1 362.0 %all-gather.8.cloned.1.call-done = bf16[1536,1,6208]{2,0,1:T(8,128)(2,1)} async-done(((bf16[192,1,6208]{2,0,1:T(8,128)(2,1)}), bf16[1536,1,6208]{2,0,1:T(8,128)(2,1)}) %all-gather.8.cloned.1.call-update) | async-done | bytes 19070992 | tf_op jit(solution)/shard_map/all_gather | solution.py:233
  392.3 9.6 mini-gather-slice.6
  401.9 8.8 gather_fusion.3
  410.7 9.2 gather_fusion.2
  419.9 17.3 maximum_select_fusion
  464.7 11.2 fusion.160
  481.7 8.4 copy-done.1
  493.8 11.2 fusion.161
  510.8 8.3 copy-done.2
  522.8 11.6 fusion.162
  540.2 8.3 copy-done.3
  552.3 10.5 fusion.163
  571.3 98.9 %reduce-scatter.5.cloned.1.call-done = f32[512,1,1536]{2,0,1:T(8,128)} async-done(((f32[2048,1,1536]{2,0,1:T(8,128)}), f32[512,1,1536]{2,0,1:T(8,128)}) %reduce-scatter.5.cloned.1.call-update) | async-done | bytes 3145744 | tf_op jit(solution)/shard_map/reduce_scatter | solution.py:131
  678.0 44.4 %all-gather.10.cloned.1.call-done = bf16[2048,1,1536]{2,0,1:T(8,128)(2,1)} async-done(((bf16[512,1,1536]{2,0,1:T(8,128)(2,1)}), bf16[2048,1,1536]{2,0,1:T(8,128)(2,1)}) %all-gather.10.cloned.1.call-update) | async-done | bytes 6291472 | tf_op jit(solution)/shard_map/all_gather | solution.py:123
  722.3 31.0 convolution_bitcast_fusion
  753.4 17.4 all-gather.12.cloned.1.call-done
  770.7 28.2 fusion.50
  799.0 30.4 fusion.45
  829.5 17.9 convolution_bitcast_fusion.1
  847.5 81.1 %reduce-scatter.9.cloned.1.call-done = f32[512,1,1536]{2,0,1:T(8,128)} async-done(((f32[2048,1,1536]{2,0,1:T(8,128)}), f32[512,1,1536]{2,0,1:T(8,128)}) %reduce-scatter.9.cloned.1.call-update) | async-done | bytes 3145744 | tf_op jit(solution)/shard_map/reduce_scatter | solution.py:140
  932.0 98.3 %reduce-scatter.7.cloned.1.call-done = f32[512,1,1536]{2,0,1:T(8,128)} async-done(((f32[2048,1,1536]{2,0,1:T(8,128)}), f32[512,1,1536]{2,0,1:T(8,128)}) %reduce-scatter.7.cloned.1.call-update) | async-done | bytes 3145744 | tf_op jit(solution)/shard_map/reduce_scatter | solution.py:131
  1037.5 45.1 %all-gather.14.cloned.1.call-done = bf16[2048,1,1536]{2,0,1:T(8,128)(2,1)} async-done(((bf16[512,1,1536]{2,0,1:T(8,128)(2,1)}), bf16[2048,1,1536]{2,0,1:T(8,128)(2,1)}) %all-gather.14.cloned.1.call-update) | async-done | bytes 6291472 | tf_op jit(solution)/shard_map/all_gather | solution.py:127
  1089.2 11.6 fusion.123
  1100.7 15.8 fusion.9
  1116.6 16.9 fusion.11
  1140.5 15.8 fusion.6
  1156.3 11.8 fusion.141
  1168.1 15.7 fusion.3
  1183.8 11.6 fusion.138
  1195.3 15.8 fusion
  1211.1 10.6 fusion.144
  1221.8 17.1 fusion.8
  1245.9 17.0 fusion.5
  1269.9 17.2 fusion.2
  1305.3 9.7 convolution_bitcast_fusion.2
  1315.8 17.9 fusion.70
  1333.8 34.2 fusion.44
  1373.7 8.8 fusion.76
  1382.5 25.1 pad_maximum_fusion
  1407.6 12.8 mini-gather-slice.9
  1420.5 15.2 mini-gather-slice.8
  1435.7 15.2 gather_fusion.1
  1450.9 15.7 gather_fusion
  1466.7 27.2 pad_maximum_fusion.1
  1493.9 27.2 bitcast_select_fusion
  1521.1 45.0 %copy.238 = f32[1536,1,6208]{2,1,0:T(1,128)} copy(f32[1536,1,6208]{2,0,1:T(8,128)} %bitcast_select_fusion) | data formatting | bytes 76283904 | tf_op jit(solution)/shard_map/jit(_take)/select_n | solution.py:384
  1589.1 43.5 %psum.7 = f32[3200]{0:T(1024)S(1)} all-reduce(f32[3200]{0:T(1024)S(1)} %concatenate.137), channel_id=1, replica_groups=mesh['dp'=8,'tensor'=4] {'dp','tensor'}, use_global_device_ids=true, to_apply=%region_38.40 | all-reduce | flops 3200 | bytes 25600 | tf_op jit(solution)/shard_map/psum | solution.py:377
  1633.2 1077.1 %all-reduce.6.cloned.1.call-done = f32[1536,1,6208]{2,1,0:T(1,128)} async-done(((f32[1536,1,6208]{2,1,0:T(1,128)}), f32[1536,1,6208]{2,1,0:T(1,128)}) %all-reduce.6.cloned.1.call-update) | async-done | bytes 38141968
  2718.2 12.4 copy.239
  2740.5 11.7 custom-call.23
  2752.3 9.8 custom-call.24
  2771.9 9.3 fusion.191
  2798.8 8.6 fusion.63
  2807.3 12.0 copy.244
  2819.3 18.1 fusion.82
  2837.5 12.2 copy.234
  2849.7 12.2 copy.241
  2861.9 14.7 fusion.54
  2884.5 12.0 copy.243
  2896.5 10.7 multiply_subtract_fusion
  2908.0 20.7 custom-call.26
  2948.4 570.4 %custom-call.27 = f32[1,1,97,64,64]{4,3,2,1,0:T(8,128)} custom-call(f32[1,1,97,64,64]{4,3,2,1,0:T(8,128)} %fusion.97), custom_call_target="Cholesky" | custom-call | tf_op jit(solution)/shard_map/jit(cholesky)/cholesky | solution.py:150
  3529.1 68.4 %custom-call.28 = f32[1,1,97,1,64,64]{2,4,5,3,1,0:T(8,128)} custom-call(f32[1,1,97,1,64,64]{2,5,4,3,1,0:T(8,128)} %select_bitcast_fusion), custom_call_target="InvertDiagBlocksLowerTriangular" | custom-call | tf_op jit(solution)/shard_map/triangular_solve | solution.py:151
  3602.5 8.2 convolution_bitcast_fusion.8
  (381 shorter events, 271.7 us)
Async XLA Ops:
  7.2 376.9 %all-gather.8.cloned.1.call-start = ((), (), s32[]{:S(2)}) async-start(), calls=%async_computation.5 | async-start | bytes 21676032 | tf_op jit(solution)/shard_map/all_gather | solution.py:233
  11.4 425.7 %all-gather.6.cloned.1.call-start = ((), (), s32[]{:S(2)}) async-start(), calls=%async_computation.4 | async-start | bytes 7864320 | tf_op jit(solution)/shard_map/all_gather | solution.py:123
  14.7 655.5 %reduce-scatter.5.cloned.1.call-start = ((), (), s32[]{:S(2)}) async-start(), calls=%async_computation.6 | async-start | bytes 15728640 | tf_op jit(solution)/shard_map/reduce_scatter | solution.py:131
  15.6 376.7 %copy-start.100 = (s32[8]{0:T(128)}, s32[8]{0:T(128)S(1)}, u32[]{:S(2)}) copy-start(s32[8]{0:T(128)S(1)} %select_reduce_fusion.3) | copy-start | bytes 100
  16.2 430.5 %copy-start.90 = (f32[64]{0:T(128)}, f32[64]{0:T(128)S(1)}, u32[]{:S(2)}) copy-start(f32[64]{0:T(128)S(1)} %get-tuple-element.194) | copy-start | bytes 772
  16.2 431.2 %copy-start.93 = (f32[64]{0:T(128)}, f32[64]{0:T(128)S(1)}, u32[]{:S(2)}) copy-start(f32[64]{0:T(128)S(1)} %get-tuple-element.193) | copy-start | bytes 772
  17.2 431.4 %copy-start.24 = (f32[2048,32]{0,1:T(8,128)}, f32[2048,32]{0,1:T(8,128)S(1)}, u32[]{:S(2)}) copy-start(f32[2048,32]{0,1:T(8,128)S(1)} %get-tuple-element.199) | copy-start | bytes 786436
  17.2 431.4 %copy-start.26 = (f32[2048,32]{0,1:T(8,128)}, f32[2048,32]{0,1:T(8,128)S(1)}, u32[]{:S(2)}) copy-start(f32[2048,32]{0,1:T(8,128)S(1)} %get-tuple-element.200) | copy-start | bytes 786436
  444.3 108.0 %copy-start.16 = (bf16[2048,1,128]{0,2,1:T(8,128)(2,1)}, bf16[2048,1,128]{0,2,1:T(8,128)(2,1)S(1)}, u32[]{:S(2)}) copy-start(bf16[2048,1,128]{0,2,1:T(8,128)(2,1)S(1)} %slice.374) | copy-start | bytes 1572868
  464.7 11.2 copy-start.65
  481.7 12.1 copy-start.67
  493.8 11.2 copy-start.69
  510.7 12.1 copy-start.71
  522.8 11.6 copy-start.73
  540.1 12.1 copy-start.75
  552.2 10.6 copy-start.77
  552.2 10.6 copy-start.46
  552.2 10.6 copy-start.48
  552.3 10.6 copy-start.50
  571.2 99.0 %copy-start.11 = (bf16[512,1,1536]{2,0,1:T(8,128)(2,1)S(1)}, bf16[512,1,1536]{2,0,1:T(8,128)(2,1)}, u32[]{:S(2)}) copy-start(bf16[512,1,1536]{2,0,1:T(8,128)(2,1)} %param.16) | copy-start | bytes 4718596
  571.3 103.0 %copy-start.57 = (f32[1536]{0:T(1024)S(1)}, f32[1536]{0:T(1024)}, u32[]{:S(2)}) copy-start(f32[1536]{0:T(1024)} %get-tuple-element.191) | copy-start | bytes 18436
  571.3 105.2 %copy-start.28 = (bf16[512,1,1536]{2,0,1:T(8,128)(2,1)S(1)}, bf16[512,1,1536]{2,0,1:T(8,128)(2,1)}, u32[]{:S(2)}) copy-start(bf16[512,1,1536]{2,0,1:T(8,128)(2,1)} %param.17) | copy-start | bytes 4718596
  571.3 151.0 %all-gather.10.cloned.1.call-start = ((), (), s32[]{:S(2)}) async-start(), calls=%async_computation.7 | async-start | bytes 7864320 | tf_op jit(solution)/shard_map/all_gather | solution.py:123
  675.8 95.0 %all-gather.12.cloned.1.call-start = ((), (), s32[]{:S(2)}) async-start(), calls=%async_computation.9 | async-start | bytes 7864320 | tf_op jit(solution)/shard_map/all_gather | solution.py:127
  677.9 250.7 %reduce-scatter.9.cloned.1.call-start = ((), (), s32[]{:S(2)}) async-start(), calls=%async_computation.10 | async-start | bytes 15728640 | tf_op jit(solution)/shard_map/reduce_scatter | solution.py:140
  829.4 200.9 %reduce-scatter.7.cloned.1.call-start = ((), (), s32[]{:S(2)}) async-start(), calls=%async_computation.8 | async-start | bytes 15728640 | tf_op jit(solution)/shard_map/reduce_scatter | solution.py:131
  847.4 81.2 %copy-start.9 = (f32[512,1,1536]{2,0,1:T(8,128)S(1)}, f32[512,1,1536]{2,0,1:T(8,128)}, u32[]{:S(2)}) copy-start(f32[512,1,1536]{2,0,1:T(8,128)} %copy-done.8) | copy-start | bytes 9437188
  847.4 81.2 %copy-start.58 = (f32[1536]{0:T(1024)S(1)}, f32[1536]{0:T(1024)}, u32[]{:S(2)}) copy-start(f32[1536]{0:T(1024)} %get-tuple-element.191) | copy-start | bytes 18436
  847.4 81.2 %copy-start.80 = (f32[512]{0:T(512)S(1)}, f32[512]{0:T(512)}, u32[]{:S(2)}) copy-start(f32[512]{0:T(512)} %copy-done.79) | copy-start | bytes 6148
  847.4 182.9 %copy-start.85 = (f32[512]{0:T(512)S(1)}, f32[512]{0:T(512)}, u32[]{:S(2)}) copy-start(f32[512]{0:T(512)} %copy-done.84) | copy-start | bytes 6148
  847.5 235.1 %all-gather.14.cloned.1.call-start = ((), (), s32[]{:S(2)}) async-start(), calls=%async_computation.11 | async-start | bytes 7864320 | tf_op jit(solution)/shard_map/all_gather | solution.py:127
  931.9 104.2 %copy-start.94 = (f32[64]{0:T(128)S(1)}, f32[64]{0:T(128)}, u32[]{:S(2)}) copy-start(f32[64]{0:T(128)} %copy-done.93) | copy-start | bytes 772
  931.9 104.8 %copy-start.91 = (f32[64]{0:T(128)S(1)}, f32[64]{0:T(128)}, u32[]{:S(2)}) copy-start(f32[64]{0:T(128)} %copy-done.90) | copy-start | bytes 772
  931.9 105.5 %copy-start.76 = (f32[2,3,512]{2,1,0:T(4,128)S(1)}, f32[2,3,512]{2,1,0:T(4,128)}, u32[]{:S(2)}) copy-start(f32[2,3,512]{2,1,0:T(4,128)} %copy-done.75) | copy-start | bytes 36868
  931.9 105.5 %copy-start.78 = (f32[2,3,512]{2,1,0:T(4,128)S(1)}, f32[2,3,512]{2,1,0:T(4,128)}, u32[]{:S(2)}) copy-start(f32[2,3,512]{2,1,0:T(4,128)} %copy-done.77) | copy-start | bytes 36868
  931.9 105.5 %copy-start.72 = (f32[2,3,512]{2,1,0:T(4,128)S(1)}, f32[2,3,512]{2,1,0:T(4,128)}, u32[]{:S(2)}) copy-start(f32[2,3,512]{2,1,0:T(4,128)} %copy-done.71) | copy-start | bytes 36868
  931.9 105.5 %copy-start.74 = (f32[2,3,512]{2,1,0:T(4,128)S(1)}, f32[2,3,512]{2,1,0:T(4,128)}, u32[]{:S(2)}) copy-start(f32[2,3,512]{2,1,0:T(4,128)} %copy-done.73) | copy-start | bytes 36868
  931.9 105.5 %copy-start.68 = (f32[2,3,512]{2,1,0:T(4,128)S(1)}, f32[2,3,512]{2,1,0:T(4,128)}, u32[]{:S(2)}) copy-start(f32[2,3,512]{2,1,0:T(4,128)} %copy-done.67) | copy-start | bytes 36868
  931.9 105.5 %copy-start.70 = (f32[2,3,512]{2,1,0:T(4,128)S(1)}, f32[2,3,512]{2,1,0:T(4,128)}, u32[]{:S(2)}) copy-start(f32[2,3,512]{2,1,0:T(4,128)} %copy-done.69) | copy-start | bytes 36868
  931.9 105.5 %copy-start.64 = (f32[2,3,512]{2,1,0:T(4,128)S(1)}, f32[2,3,512]{2,1,0:T(4,128)}, u32[]{:S(2)}) copy-start(f32[2,3,512]{2,1,0:T(4,128)} %copy-done.63) | copy-start | bytes 36868
  931.9 105.5 %copy-start.66 = (f32[2,3,512]{2,1,0:T(4,128)S(1)}, f32[2,3,512]{2,1,0:T(4,128)}, u32[]{:S(2)}) copy-start(f32[2,3,512]{2,1,0:T(4,128)} %copy-done.65) | copy-start | bytes 36868
  1036.0 542.2 %reduce-scatter.11.cloned.1.call-start = ((), (), s32[]{:S(2)}) async-start(), calls=%async_computation.12 | async-start | bytes 15728640 | tf_op jit(solution)/shard_map/reduce_scatter | solution.py:140
  1089.1 11.6 copy-start.17
  1116.5 16.9 copy-start.32
  1315.0 18.7 slice-start.4
  1315.0 1395.3 %all-reduce.6.cloned.1.call-start = ((), (), s32[]{:S(2)}) async-start(), calls=%async_computation.13 | async-start | bytes 77070336
  1315.8 17.9 slice-start.5
  1333.7 34.2 copy-start.47
  1333.7 34.2 copy-start.49
  1333.8 34.2 copy-start.51
  1333.8 34.2 copy-start.53
  1566.1 10.6 copy-start.102
  1566.2 11.9 copy-start.89
  1566.2 12.0 copy-start.98
  1566.2 12.1 copy-start.12
  1566.2 12.1 copy-start.60
  1566.2 12.1 copy-start.83
  1581.2 51.3 %copy-start.62 = (f32[3200]{0:T(1024)S(1)}, f32[3200]{0:T(1024)}, u32[]{:S(2)}) copy-start(f32[3200]{0:T(1024)} %param.27) | copy-start | bytes 38404
  1581.3 51.3 %copy-start.86 = (f32[3200]{0:T(1024)S(1)}, f32[3200]{0:T(1024)}, u32[]{:S(2)}) copy-start(f32[3200]{0:T(1024)} %param.29) | copy-start | bytes 38404
  1581.3 51.3 %copy-start.87 = (f32[3200]{0:T(1024)S(1)}, f32[3200]{0:T(1024)}, u32[]{:S(2)}) copy-start(f32[3200]{0:T(1024)} %param.28) | copy-start | bytes 38404
  2718.2 21.0 copy-start.44
  2771.2 10.0 slice-start
  2861.9 14.7 copy-start.5
  3602.5 12.3 copy-start.39
  (55 other events, 207.9 us)
Sparse Core Ops, SparseCore 0:
  11.6 372.5 all-gather.7
  386.3 46.3 all-gather.5
  571.4 98.8 reduce-scatter.4
  675.9 46.3 all-gather.9
  724.3 46.3 all-gather.11
  829.6 99.0 reduce-scatter.8
  931.2 99.0 reduce-scatter.6
  1036.1 46.3 all-gather.13
  1315.2 99.0 reduce-scatter.10
  1566.3 1143.9 all-reduce.5
where the time goes:
time: 3630 us; the launch traced here: 3620 us
  waiting for transfers between devices  1820 us (50%)
  other arithmetic  950 us (26%)
  matrix products  488 us (13%)
  local copies, waits for them, and re-layouts  297 us (8%)
  blocking collectives  43.5 us (1%)
    unnamed x11, waiting for transfers between devices  1080 us
    another operation x11, other arithmetic, orthonormal(): factor = jnp.linalg.cholesky(gram_matrix)  601 us
    all_gather x1, waiting for transfers between devices, body(): joined_w = arrange(lax.all_gather(weight_low, 'dp', axis=0, tiled=True))  362 us
    reduce_scatter x2, waiting for transfers between devices, branch_sum(): lax.psum_scatter(jnp.einsum('tsc,dc->tsd', left_rows, right_w, preferred_...  197 us
    another operation x9, other arithmetic, orthonormal(): lax.linalg.triangular_solve(factor, matrix, left_side=False, lower=True,...  94.1 us
    reduce_scatter x2, waiting for transfers between devices, input_sum(): lax.psum_scatter(jnp.einsum('tsc,dc->tsd', left_rows, right_w, preferred_...  81.1 us
    unnamed x228, local copies, waits for them, and re-layouts  73.2 us
  transfers between devices with their start and end apart: 10, of which 8 were waited for; matrix products, arithmetic and copies ran while one was open for 11% of the time, Pallas kernels for 0%

commit v1 on v0

v1 whole, which is shorter than its diff:
```python
import functools

import jax
import jax.numpy as jnp
from jax import lax
from jax.experimental import pallas as pl
from jax.experimental.pallas import tpu as pltpu
from jax.sharding import PartitionSpec as P

MODEL_DIM = 1536
QUERY_HEADS = 24
KEY_VALUE_HEADS = 8
HEAD_DIM = 64
FF = 6912
STEP = 10

NORM_EPS = 1e-06
ROPE_THETA = 1000000.0
MOMENT_DECAY = 0.5
ADAM_EPSILON = 1e-08
RATE_WEIGHT = 0.05
RATE_GAIN = 0.3
DECAY_WEIGHT = 0.01
MASKED_SCORE = -1e30
PRECISE = lax.Precision.HIGHEST
F32 = jnp.float32
BF16 = jnp.bfloat16
VMEM_LIMIT = 60 * 1024 * 1024
NT = (((1,), (1,)), ((), ()))
TN = (((0,), (0,)), ((), ()))


def params(*kinds):
    return pltpu.CompilerParams(dimension_semantics=kinds, vmem_limit_bytes=VMEM_LIMIT)


def rms_rows(values, gain_vec):
    inverse = lax.rsqrt(jnp.mean(values * values, axis=-1, keepdims=True) + NORM_EPS)
    scaled = values * inverse
    return (scaled * gain_vec, scaled, inverse)


def norm_back(grad_norm, scaled, inverse, gain_vec):
    grad_scaled = grad_norm * gain_vec
    row_inner = jnp.mean(grad_scaled * scaled, axis=-1, keepdims=True)
    return inverse * (grad_scaled - scaled * row_inner)


def rope_tables(positions_count):
    half_dim = HEAD_DIM // 2
    frequency = ROPE_THETA ** (-(jnp.arange(half_dim, dtype=F32) * 2.0 / HEAD_DIM))
    angles = jnp.arange(positions_count, dtype=F32)[:, None] * frequency[None, :]
    return (jnp.cos(angles), jnp.sin(angles))


def lane_tables(positions_count):
    cosine, sine = rope_tables(positions_count)
    return jnp.concatenate([cosine] * 4, axis=1), jnp.concatenate([-sine, sine] * 2, axis=1)


def lanes_like(values):
    return lax.broadcasted_iota(jnp.int32, values.shape, 1)


def both_sums(values):
    low = lanes_like(values) < HEAD_DIM
    first = jnp.sum(jnp.where(low, values, 0.0), axis=1, keepdims=True)
    second = jnp.sum(jnp.where(low, 0.0, values), axis=1, keepdims=True)
    return jnp.where(low, first, second)


def turned(values):
    low = (lanes_like(values) & (HEAD_DIM - 1)) < HEAD_DIM // 2
    return jnp.where(low, pltpu.roll(values, 96, 1), pltpu.roll(values, 32, 1))


def pair_inverse(values):
    return lax.rsqrt(both_sums(values * values) * (1.0 / HEAD_DIM) + NORM_EPS)


def only(head, values):
    low = lanes_like(values) < HEAD_DIM
    zero = jnp.zeros_like(values)
    return jnp.where(low, zero, values) if head % 2 else jnp.where(low, values, zero)


def twice(values):
    low = lanes_like(values) < HEAD_DIM
    other = pltpu.roll(values, HEAD_DIM, 1)
    return jnp.where(low, values, other), jnp.where(low, other, values)


MESH_ID = pl.DeviceIdType.MESH
DMA = pltpu.SemaphoreType.DMA
HBM = pl.BlockSpec(memory_space=pl.ANY)


def one_buffer(shape):
    zeros = (0,) * len(shape)
    return pl.BlockSpec(shape, lambda *_: zeros, pipeline_mode=pl.Buffered(1))


def ring_index(place, count):
    place = lax.rem(place + 2 * count, count)
    odd = lax.div(place, count // 2)
    return 2 * place * (1 - odd) + (2 * (count - 1 - place) + 1) * odd


def ring_place(count):
    me = lax.axis_index("dp")
    odd = lax.rem(me, 2)
    half = lax.div(me, 2)
    return half * (1 - odd) + (count - 1 - half) * odd


def ring_neighbours(count):
    place = ring_place(count)
    return [{"dp": ring_index(place + 1, count)}, {"dp": ring_index(place - 1, count)}]


def tensor_ranks():
    rank = lax.axis_index("tensor")
    core, chip = lax.rem(rank, 2), lax.div(rank, 2)
    return (
        rank,
        2 * chip + 1 - core,
        2 * (1 - chip) + core,
        2 * (1 - chip) + 1 - core,
    )


def greet(peers):
    barrier = pltpu.get_barrier_semaphore()
    for peer in peers:
        pl.semaphore_signal(barrier, inc=1, device_id=peer, device_id_type=MESH_ID)
    pl.semaphore_wait(barrier, len(peers))


def tensor_peers():
    _, pair, across, _ = tensor_ranks()
    return [{"tensor": pair}, {"tensor": across}]


def remote(src, dst, send, recv, peer):
    return pltpu.make_async_remote_copy(
        src_ref=src, dst_ref=dst, send_sem=send, recv_sem=recv, device_id=peer, device_id_type=MESH_ID
    )


def row_parts(rows, pieces):
    units = rows // 16
    forward = (units + 1) // 2
    parts = []
    for way, start, size in ((0, 0, forward), (1, forward, units - forward)):
        cuts = [start + size * i // pieces for i in range(pieces + 1)]
        parts += [(way, 16 * lo, 16 * (hi - lo)) for lo, hi in zip(cuts, cuts[1:]) if hi > lo]
    return parts


class RingGather:
    PIECES = 2

    @classmethod
    def scratch(cls, count, rows):
        return [DMA((2, len(row_parts(rows, cls.PIECES)), count - 1)), DMA((1,))]

    def __init__(self, count, shard, whole, sems, local):
        self.count, self.shard, self.whole, self.sems = count, shard, whole, sems
        self.parts = row_parts(shard.shape[0], self.PIECES)
        self.place = ring_place(count)
        self.peers = ring_neighbours(count)
        self.own = pltpu.make_async_copy(shard, whole.at[lax.axis_index("dp")], local.at[0])

    def out(self, step, index):
        way, start, size = self.parts[index]
        block = ring_index(self.place + (step if way else -step), self.count)
        where = self.whole.at[block, pl.ds(start, size)]
        src = self.shard.at[pl.ds(start, size)] if step == 0 else where
        return remote(
            src, where, self.sems.at[0, index, step], self.sems.at[1, index, step], self.peers[way]
        )

    def into(self, step, index):
        way, start, size = self.parts[index]
        block = ring_index(self.place + (step + 1 if way else -step - 1), self.count)
        where = self.whole.at[block, pl.ds(start, size)]
        return remote(
            where, where, self.sems.at[0, index, step], self.sems.at[1, index, step], self.peers[way]
        )

    def begin(self):
        self.own.start()
        for index in range(len(self.parts)):
            self.out(0, index).start()

    def step(self, step):
        for index in range(len(self.parts)):
            self.into(step, index).wait_recv()
            if step < self.count - 2:
                self.out(step + 1, index).start()

    def finish(self):
        self.own.wait()
        for step in range(self.count - 1):
            for index in range(len(self.parts)):
                self.out(step, index).wait_send()


class RingScatter:
    PIECES = 2

    @classmethod
    def scratch(cls, count, rows, cols, loads=True):
        parts = len(row_parts(rows, cls.PIECES))
        slots = [pltpu.VMEM((count - 1, rows, cols), BF16), DMA((2, parts, count - 1))]
        return slots + ([pltpu.VMEM((2, rows, cols), BF16), DMA((parts, count - 1))] if loads else [])

    def __init__(self, count, take, out, slots, sems, held=None, load_sems=None):
        self.count, self.take, self.out_ref = count, take, out
        self.slots, self.sems, self.held, self.load_sems = slots, sems, held, load_sems
        self.parts = row_parts(slots.shape[1], self.PIECES)
        self.place = ring_place(count)
        self.peers = ring_neighbours(count)

    def local(self, step, index):
        way, start, size = self.parts[index]
        block = ring_index(self.place + (step + 1 if way else -step - 1), self.count)
        return self.take(block, start, size)

    def load(self, step, index):
        _, start, size = self.parts[index]
        return pltpu.make_async_copy(
            self.local(step + 1, index),
            self.held.at[step % 2, pl.ds(start, size)],
            self.load_sems.at[index, step],
        )

    def out(self, step, index):
        way, start, size = self.parts[index]
        rows = pl.ds(start, size)
        return remote(
            self.local(0, index) if step == 0 else self.slots.at[step - 1, rows],
            self.slots.at[step, rows],
            self.sems.at[0, index, step],
            self.sems.at[1, index, step],
            self.peers[way],
        )

    def begin(self):
        for index in range(len(self.parts)):
            self.out(0, index).start()
            if self.held is not None:
                for step in range(min(2, self.count - 1)):
                    self.load(step, index).start()

    def step(self, step):
        for index, (way, start, size) in enumerate(self.parts):
            rows = pl.ds(start, size)
            if self.held is None:
                local = self.local(step + 1, index)[...]
            else:
                self.load(step, index).wait()
                local = self.held[step % 2, rows]
            self.out(step, index).wait_recv()
            total = self.slots[step, rows].astype(F32) + local.astype(F32)
            if step == self.count - 2:
                self.out_ref[rows] = total
            else:
                self.slots[step, rows] = total.astype(BF16)
                self.out(step + 1, index).start()
            if self.held is not None and step + 2 < self.count - 1:
                self.load(step + 2, index).start()

    def finish(self):
        for step in range(self.count - 1):
            for index in range(len(self.parts)):
                self.out(step, index).wait_send()


def rows_of(grads, first=0):
    return lambda block, start, size: grads.at[block, pl.ds(first + start, size)]


CHUNKS = 4


class Exchange:
    @staticmethod
    def scratch(rows, cols):
        return [pltpu.VMEM((rows, cols), BF16)] * 5 + [DMA((8, CHUNKS))]

    def __init__(self, parts, to_send, mine, slot_a, slot_b, slot_x, sems):
        self.parts, self.sems = parts, sems
        self.to_send, self.mine = to_send, mine
        self.slot_a, self.slot_b, self.slot_x = slot_a, slot_b, slot_x
        self.size = mine.shape[0] // CHUNKS
        self.ranks = tensor_ranks()
        self.pair, self.across = tensor_peers()

    def rows(self, k):
        return pl.ds(k * self.size, self.size)

    def load_send(self, k):
        rows = self.rows(k)
        return pltpu.make_async_copy(
            self.parts.at[self.ranks[2], rows], self.to_send.at[rows], self.sems.at[0, k]
        )

    def load_mine(self, k):
        rows = self.rows(k)
        return pltpu.make_async_copy(
            self.parts.at[self.ranks[0], rows], self.mine.at[rows], self.sems.at[1, k]
        )

    def copy_a(self, k):
        rows = self.rows(k)
        return remote(
            self.parts.at[self.ranks[3], rows], self.slot_a.at[rows],
            self.sems.at[2, k], self.sems.at[3, k], self.pair,
        )

    def copy_b(self, k):
        rows = self.rows(k)
        return remote(
            self.parts.at[self.ranks[1], rows], self.slot_b.at[rows],
            self.sems.at[4, k], self.sems.at[5, k], self.pair,
        )

    def copy_x(self, k):
        rows = self.rows(k)
        return remote(
            self.to_send.at[rows], self.slot_x.at[rows],
            self.sems.at[6, k], self.sems.at[7, k], self.across,
        )

    def begin(self):
        for k in range(CHUNKS):
            self.load_send(k).start()
            self.copy_a(k).start()
        for k in range(CHUNKS):
            self.load_mine(k).start()
            self.copy_b(k).start()

    def forward(self, k):
        self.load_send(k).wait()
        self.copy_a(k).wait_recv()
        rows = self.rows(k)
        self.to_send[rows] = (
            self.to_send[rows].astype(F32) + self.slot_a[rows].astype(F32)
        ).astype(BF16)
        self.copy_x(k).start()

    def result(self, k):
        self.load_mine(k).wait()
        self.copy_b(k).wait_recv()
        self.copy_x(k).wait_recv()
        rows = self.rows(k)
        return (
            self.mine[rows].astype(F32) + self.slot_b[rows].astype(F32)
        ) + self.slot_x[rows].astype(F32)

    def finish(self):
        for k in range(CHUNKS):
            self.copy_a(k).wait_send()
            self.copy_b(k).wait_send()
            self.copy_x(k).wait_send()


class Spread:
    @staticmethod
    def scratch():
        return [DMA((7, CHUNKS))]

    def __init__(self, own, whole, sems):
        self.own, self.whole, self.sems = own, whole, sems
        self.size = own.shape[0] // CHUNKS
        self.ranks = tensor_ranks()
        self.pair, self.across = tensor_peers()

    def rows(self, k):
        return pl.ds(k * self.size, self.size)

    def local(self, k):
        rows = self.rows(k)
        return pltpu.make_async_copy(
            self.own.at[rows], self.whole.at[self.ranks[0], rows], self.sems.at[0, k]
        )

    def to_peer(self, k, kind):
        rows = self.rows(k)
        return remote(
            self.own.at[rows], self.whole.at[self.ranks[0], rows],
            self.sems.at[1 + 2 * kind, k], self.sems.at[2 + 2 * kind, k],
            self.across if kind else self.pair,
        )

    def on(self, k):
        rows = self.rows(k)
        where = self.whole.at[self.ranks[2], rows]
        return remote(where, where, self.sems.at[5, k], self.sems.at[6, k], self.pair)

    def send(self, k):
        self.to_peer(k, 1).start()
        self.to_peer(k, 0).start()
        self.local(k).start()

    def forward(self, k):
        self.to_peer(k, 1).wait_recv()
        self.on(k).start()

    def finish(self):
        for k in range(CHUNKS):
            self.local(k).wait()
            self.to_peer(k, 0).wait()
            self.to_peer(k, 1).wait_send()
            self.on(k).wait()


def timed(calls, first, last):
    gap = (last - first) / max(len(calls) - 1, 1)
    return [(first + i * gap, call) for i, call in enumerate(calls)]


def merge(*lists):
    for _, call in sorted(sum(lists, []), key=lambda entry: entry[0]):
        call()


def at_grid(now, ends, *lists):
    plan = {}
    for time, call in sorted(sum(lists, []), key=lambda entry: entry[0]):
        when = next((i for i, end in enumerate(ends) if end >= time), len(ends) - 1)
        plan.setdefault(when, []).append(call)
    for when, calls in plan.items():

        @pl.when(now == when)
        def _(calls=calls):
            for call in calls:
                call()


def comm_params(ident):
    return pltpu.CompilerParams(
        collective_id=ident, has_side_effects=True, vmem_limit_bytes=VMEM_LIMIT
    )


def steps_of(ring, gap, start=0.0):
    gap = gap * 7 / (ring.count - 1)
    return [
        (start + gap * (s + 1), functools.partial(ring.step, s)) for s in range(ring.count - 1)
    ]


def front_kernel(count, a_ref, wa_ref, a_all, wa_all, *scratch):
    greet(tensor_peers() + ring_neighbours(count))
    ring = RingGather(count, wa_ref, wa_all, *scratch[0:2])
    spread = Spread(a_ref, a_all, scratch[2])
    ring.begin()
    for k in range(CHUNKS):
        spread.send(k)
    moves = [functools.partial(spread.forward, k) for k in range(CHUNKS)]
    merge(steps_of(ring, 4.2), timed(moves, 20, 32))
    ring.finish()
    spread.finish()


def front(count, normed, w_attn):
    rows, width = normed.shape
    shape = jax.ShapeDtypeStruct
    return pl.pallas_call(
        functools.partial(front_kernel, count),
        in_specs=[HBM] * 2,
        out_specs=[HBM] * 2,
        out_shape=[shape((4, rows, width), BF16), shape((count,) + w_attn.shape, BF16)],
        scratch_shapes=RingGather.scratch(count, w_attn.shape[0]) + Spread.scratch(),
        compiler_params=comm_params(1),
        name="front",
    )(normed, w_attn)


def rms_of(values):
    return lax.rsqrt(jnp.mean(values * values, axis=-1, keepdims=True) + NORM_EPS)


def middle_kernel(count, part, x_ref, g_ref, wu_ref, wd_ref, h_ref, a_all, wu_all, wd_all, own, *scratch):
    greet(tensor_peers() + ring_neighbours(count))
    exchange = Exchange(part, *scratch[0:6])
    spread = Spread(own, a_all, scratch[6])
    ring_u = RingGather(count, wu_ref, wu_all, *scratch[7:9])
    ring_d = RingGather(count, wd_ref, wd_all, *scratch[9:11])
    exchange.begin()
    ring_u.begin()
    ring_d.begin()

    def land(k):
        rows = exchange.rows(k)
        value = x_ref[rows].astype(F32) + exchange.result(k)
        h_ref[rows] = value
        own[rows] = (value * rms_of(value) * g_ref[...]).astype(BF16)
        spread.send(k)

    def each(call):
        return [functools.partial(call, k) for k in range(CHUNKS)]

    merge(
        timed(each(exchange.forward), 0, 1),
        timed(each(land), 30, 34),
        timed(each(spread.forward), 62, 66),
        steps_of(ring_u, 10.5),
        steps_of(ring_d, 10.5),
    )
    for item in (exchange, spread, ring_u, ring_d):
        item.finish()


def middle(count, part, x, gain, shard_u, shard_d):
    rows, width = x.shape
    shape = jax.ShapeDtypeStruct
    vmem = pl.BlockSpec(memory_space=pltpu.VMEM)
    return pl.pallas_call(
        functools.partial(middle_kernel, count),
        in_specs=[HBM, vmem, vmem, HBM, HBM],
        out_specs=[vmem, HBM, HBM, HBM],
        out_shape=[
            shape((rows, width), F32),
            shape((4, rows, width), BF16),
            shape((count,) + shard_u.shape, BF16),
            shape((count,) + shard_d.shape, BF16),
        ],
        scratch_shapes=[pltpu.VMEM((rows, width), BF16)]
        + Exchange.scratch(rows, width)
        + Spread.scratch()
        + RingGather.scratch(count, shard_u.shape[0])
        + RingGather.scratch(count, shard_d.shape[0]),
        compiler_params=comm_params(2),
        name="middle",
    )(part, x, gain, shard_u, shard_d)


def feed_forward_kernel(a_ref, dy_ref, wg_ref, wu_ref, wd_ref, hid_ref, da_ref, acc):
    cols = wg_ref.shape[1]
    a2, dy = a_ref[...], dy_ref[...]
    for start in range(0, cols, 256):
        part = slice(start, min(start + 256, cols))
        wg, wu = wg_ref[:, part], wu_ref[:, part]
        gate = jnp.dot(a2, wg, preferred_element_type=F32)
        up = jnp.dot(a2, wu, preferred_element_type=F32)
        grad = jnp.dot(dy, wd_ref[:, part], preferred_element_type=F32)
        sig = jax.nn.sigmoid(gate)
        silu = gate * sig
        hid_ref[0, :, part] = (silu * up).astype(BF16)
        d_gate = (grad * up * sig * (1.0 + gate * (1.0 - sig))).astype(BF16)
        d_up = (grad * silu).astype(BF16)
        hid_ref[1, :, part] = d_gate
        hid_ref[2, :, part] = d_up
        back = lax.dot_general(d_gate, wg, NT, preferred_element_type=F32) + lax.dot_general(
            d_up, wu, NT, preferred_element_type=F32
        )
        if start == 0:
            acc[...] = back
        else:
            acc[...] += back
    da_ref[...] = acc[...].astype(BF16)


FF_ROWS = 512


def feed_forward(a2, dy, w_gate, w_up, w_down):
    seq, width = a2.shape
    cols = w_gate.shape[1]
    rows = pl.BlockSpec((FF_ROWS, width), lambda i: (i, 0))
    return pl.pallas_call(
        feed_forward_kernel,
        grid=(seq // FF_ROWS,),
        in_specs=[rows, rows] + [one_buffer((width, cols))] * 3,
        out_specs=[pl.BlockSpec((3, FF_ROWS, cols), lambda i: (0, i, 0)), rows],
        out_shape=[
            jax.ShapeDtypeStruct((3, seq, cols), BF16),
            jax.ShapeDtypeStruct((seq, width), BF16),
        ],
        scratch_shapes=[pltpu.VMEM((FF_ROWS, width), F32)],
        compiler_params=params("arbitrary"),
        cost_estimate=pl.CostEstimate(
            flops=10 * seq * width * cols, bytes_accessed=8 * seq * (width + cols), transcendentals=seq * cols
        ),
        name="feed_forward",
    )(a2, dy, w_gate, w_up, w_down)


M_COLS = 256


def turn_kernel(
    count, own_rows, ff_steps, dyt_ref, a_ref, rhs_ref, hid_ref, w_ref, part, h_ref, dy_ref, g_ref,
    dgu_ref, ffn_ref, d_ref, gain_ref, z_all, sum_ref, own, d_down, *scratch
):
    now = pl.program_id(0)
    cuts = w_ref.shape[0] // M_COLS
    exchange = Exchange(part, *scratch[0:6])
    spread = Spread(own, z_all, scratch[6])

    def take(block, start, size):
        return d_down.at[pl.ds(pl.multiple_of(block * own_rows + start, 16), size)]

    ring = RingScatter(count, take, sum_ref, *scratch[7:9])

    @pl.when(now == 0)
    def _():
        greet(tensor_peers() + ring_neighbours(count))
        exchange.begin()
        gain_ref[...] = jnp.zeros_like(gain_ref)

    @pl.when(now < cuts)
    def _():
        at = pl.multiple_of(now * M_COLS, M_COLS)
        d_down[pl.ds(at, M_COLS)] = lax.dot_general(
            dyt_ref[...], rhs_ref[0], TN, preferred_element_type=F32
        ).astype(BF16)

    @pl.when((now >= cuts) & (now < 3 * cuts))
    def _():
        dgu_ref[0] = lax.dot_general(
            a_ref[...], rhs_ref[0], TN, preferred_element_type=F32
        ).astype(BF16)

    @pl.when(now >= 3 * cuts)
    def _():
        ffn_ref[...] = lax.dot_general(
            hid_ref[0], w_ref[...], NT, preferred_element_type=F32
        ).astype(BF16)

    def land(k):
        rows = exchange.rows(k)
        grad = exchange.result(k)
        value = h_ref[rows]
        inverse = rms_of(value)
        scaled = value * inverse
        gain_ref[...] += jnp.sum(grad * scaled, axis=0, keepdims=True)
        back = dy_ref[rows].astype(F32) + norm_back(grad, scaled, inverse, g_ref[...])
        d_ref[rows] = back
        own[rows] = back.astype(BF16)
        spread.send(k)

    def each(call):
        return [functools.partial(call, k) for k in range(CHUNKS)]

    total = 3 * cuts + ff_steps
    ends = [2.7 * (i + 1) for i in range(total)]
    at_grid(
        now,
        ends,
        timed(each(exchange.forward), 3, 3),
        timed(each(land), 33, 36),
        timed(each(spread.forward), 66, 69),
        [(ends[cuts - 1], ring.begin)],
        steps_of(ring, 7.0, ends[cuts - 1]),
    )

    @pl.when(now == total - 1)
    def _():
        for item in (exchange, spread, ring):
            item.finish()


def turn(count, part, h, dy, gain, dy_all, a_all, hidden3, w_down):
    rows, width = h.shape
    _, seq, cols = hidden3.shape
    own = width // count
    cuts = width // M_COLS
    ff_rows = 256
    ff_steps = seq // ff_rows
    shape = jax.ShapeDtypeStruct

    def within(i, low, high):
        return jnp.minimum(jnp.maximum(i - low, 0), high)

    def gu_block(i):
        at = within(i, cuts, 2 * cuts - 1)
        return lax.div(at, cuts), lax.rem(at, cuts)

    def ff_block(i):
        return within(i, 3 * cuts, ff_steps - 1)

    return pl.pallas_call(
        functools.partial(turn_kernel, count, own, ff_steps),
        grid=(3 * cuts + ff_steps,),
        in_specs=[
            pl.BlockSpec((seq, M_COLS), lambda i: (0, within(i, 0, cuts - 1))),
            pl.BlockSpec((seq, M_COLS), lambda i: (0, gu_block(i)[1])),
            pl.BlockSpec(
                (1, seq, cols),
                lambda i: (jnp.minimum(lax.div(i, cuts), 2), 0, 0),
                pipeline_mode=pl.Buffered(1),
            ),
            pl.BlockSpec((1, ff_rows, cols), lambda i: (0, ff_block(i), 0)),
            one_buffer(w_down.shape),
            HBM,
            one_buffer(h.shape),
            one_buffer(h.shape),
            one_buffer(gain.shape),
        ],
        out_specs=[
            pl.BlockSpec((1, M_COLS, cols), lambda i: gu_block(i) + (0,)),
            pl.BlockSpec((ff_rows, width), lambda i: (ff_block(i), 0)),
            one_buffer(h.shape),
            one_buffer(gain.shape),
            HBM,
            one_buffer((own, cols)),
        ],
        out_shape=[
            shape((2, width, cols), BF16),
            shape((seq, width), BF16),
            shape((rows, width), F32),
            shape((1, width), F32),
            shape((4, rows, width), BF16),
            shape((own, cols), F32),
        ],
        scratch_shapes=[pltpu.VMEM((rows, width), BF16), pltpu.VMEM((width, cols), BF16)]
        + Exchange.scratch(rows, width)
        + Spread.scratch()
        + RingScatter.scratch(count, own, cols, loads=False),
        compiler_params=comm_params(3),
        name="turn",
    )(dy_all, a_all, hidden3, hidden3, w_down, part, h, dy, gain)


def last_kernel(
    count, first, part, x_ref, d_ref, g_ref, grads_u, grads_a, out_ref, gain_ref, sum_u, sum_a, *scratch
):
    greet(tensor_peers() + ring_neighbours(count))
    exchange = Exchange(part, *scratch[0:6])
    ring_u = RingScatter(count, rows_of(grads_u.at[1], first), sum_u, *scratch[6:10])
    ring_a = RingScatter(count, rows_of(grads_a), sum_a, *scratch[10:14])
    exchange.begin()
    ring_u.begin()
    ring_a.begin()
    gain_ref[...] = jnp.zeros_like(gain_ref)

    def land(k):
        rows = exchange.rows(k)
        grad = exchange.result(k)
        value = x_ref[rows].astype(F32)
        inverse = rms_of(value)
        scaled = value * inverse
        gain_ref[...] += jnp.sum(grad * scaled, axis=0, keepdims=True)
        out_ref[rows] = d_ref[rows] + norm_back(grad, scaled, inverse, g_ref[...])

    def each(call):
        return [functools.partial(call, k) for k in range(CHUNKS)]

    merge(
        timed(each(exchange.forward), 0, 1),
        timed(each(land), 33, 36),
        steps_of(ring_u, 7.6),
        steps_of(ring_a, 7.6),
    )
    for item in (exchange, ring_u, ring_a):
        item.finish()


def last(count, part, x, d, gain, grads_u, first, grads_a):
    rows, width = x.shape
    _, _, own, cols = grads_u.shape
    shape = jax.ShapeDtypeStruct
    vmem = pl.BlockSpec(memory_space=pltpu.VMEM)
    return pl.pallas_call(
        functools.partial(last_kernel, count, first),
        in_specs=[HBM, vmem, vmem, vmem, HBM, HBM],
        out_specs=[vmem, vmem, vmem, vmem],
        out_shape=[
            shape((rows, width), F32),
            shape((1, width), F32),
            shape((own - first, cols), F32),
            shape(grads_a.shape[1:], F32),
        ],
        scratch_shapes=Exchange.scratch(rows, width)
        + RingScatter.scratch(count, own - first, cols)
        + RingScatter.scratch(*grads_a.shape),
        compiler_params=comm_params(4),
        name="last",
    )(part, x, d, gain, grads_u, grads_a)


GROUPS = 2
GROUP = QUERY_HEADS // KEY_VALUE_HEADS
HEADS = GROUPS * GROUP
Q_COLS = HEADS * HEAD_DIM
QK_COLS = Q_COLS + GROUPS * HEAD_DIM
QKV_COLS = QK_COLS + GROUPS * HEAD_DIM
Q_ROWS = 256
K_STEP = 512


def pair_of(head):
    return slice(128 * (head // 2), 128 * (head // 2) + 128)


def attend_kernel(
    count, blocks, a_ref, w_ref, gq_ref, gk_ref, cos_ref, sin_ref, bias_ref, dy_ref, wg_ref, wd_ref,
    part_ref, q_ref, k_ref, v_ref, raw_ref, o_ref, lse_ref, dy_all, wg_all, wd_all,
    k_scr, v_scr, s_scr, m_scr, l_scr, acc_scr, *scratch
):
    rows = a_ref.shape[0]
    seq = k_scr.shape[1]
    step = min(K_STEP, seq)
    tall = GROUP * rows
    block = pl.program_id(0)
    ends = [5.0 + 2.1 * (1 + (i * rows) // step) for i in range(blocks)]
    ends = [sum(ends[: i + 1]) for i in range(len(ends))]
    ring_g = RingGather(count, wg_ref, wg_all, *scratch[0:2])
    ring_d = RingGather(count, wd_ref, wd_all, *scratch[2:4])
    spread = Spread(dy_ref, dy_all, scratch[4])

    @pl.when(block == 0)
    def _():
        k_scr[...] = jnp.zeros_like(k_scr)
        v_scr[...] = jnp.zeros_like(v_scr)
        greet(tensor_peers() + ring_neighbours(count))
        ring_g.begin()
        ring_d.begin()
        for k in range(CHUNKS):
            spread.send(k)

    raw = jnp.dot(a_ref[...], w_ref[:, :QKV_COLS], preferred_element_type=F32)
    raw_ref[...] = raw[:, :QK_COLS]
    cosine, sine = cos_ref[...], sin_ref[...]

    def roped(values, gain):
        normed = values * pair_inverse(values) * gain
        return normed * cosine + turned(normed) * sine

    for head in range(0, HEADS, 2):
        q_ref[:, pair_of(head)] = roped(raw[:, pair_of(head)], gq_ref[...]).astype(
            BF16
        ) * HEAD_DIM ** (-0.5)
    key = roped(raw[:, Q_COLS:QK_COLS], gk_ref[...])
    value = raw[:, QK_COLS:]
    k_ref[...] = key.astype(BF16)
    v_ref[...] = value.astype(BF16)
    here = pl.ds(pl.multiple_of(block * rows, rows), rows)
    for group, (one_key, one_value) in enumerate(zip(twice(key), twice(value))):
        k_scr[group, here] = one_key.astype(BF16)
        v_scr[group, here] = one_value.astype(BF16)

    last_block = lax.div(block * rows, step)
    at_last = pl.multiple_of(last_block * step, step)
    for group in range(GROUPS):
        heads = range(group * GROUP, group * GROUP + GROUP)
        query = jnp.concatenate([only(head, q_ref[:, pair_of(head)]) for head in heads], axis=0)
        m_scr[...] = jnp.full_like(m_scr, MASKED_SCORE)
        l_scr[...] = jnp.zeros_like(l_scr)
        acc_scr[group] = jnp.zeros_like(acc_scr[group])

        def scores(at, group=group, query=query):
            keys = k_scr[group, pl.ds(at, step), :]
            return lax.dot_general(query, keys, NT, preferred_element_type=F32) + bias_ref[
                :, pl.ds(at, step)
            ]

        def keep(at, found):
            s_scr[:, pl.ds(at, step)] = found
            top = found[:, :128]
            for part in range(1, step // 128):
                top = jnp.maximum(top, found[:, part * 128 : (part + 1) * 128])
            m_scr[...] = jnp.maximum(m_scr[...], top)

        @pl.loop(0, last_block)
        def _(index, scores=scores, keep=keep):
            at = pl.multiple_of(index * step, step)
            keep(at, scores(at))

        found = scores(at_last)
        row_pos = block * rows + (lax.broadcasted_iota(jnp.int32, (tall, step), 0) & (rows - 1))
        key_pos = at_last + lax.broadcasted_iota(jnp.int32, (tall, step), 1)
        keep(at_last, jnp.where(key_pos <= row_pos, found, MASKED_SCORE))
        top = jnp.max(m_scr[...], axis=1, keepdims=True)

        @pl.loop(0, last_block + 1)
        def _(index, group=group, top=top):
            at = pl.multiple_of(index * step, step)
            prob = jnp.exp(s_scr[:, pl.ds(at, step)] - top)
            total = prob[:, :128]
            for part in range(1, step // 128):
                total = total + prob[:, part * 128 : (part + 1) * 128]
            l_scr[...] += total
            acc_scr[group] += jnp.dot(
                prob.astype(BF16), v_scr[group, pl.ds(at, step), :], preferred_element_type=F32
            )

        total = jnp.sum(l_scr[...], axis=1, keepdims=True)
        acc_scr[group] = acc_scr[group] / total
        lse = jnp.broadcast_to(top + jnp.log(total), (tall, 128)).T[0:1, :]
        for i, head in enumerate(heads):
            lse_ref[head : head + 1, :] = lse[:, i * rows : (i + 1) * rows]

    def head_out(head):
        at = (head % GROUP) * rows
        return acc_scr[head // GROUP, at : at + rows, :]

    for head in range(0, HEADS, 2):
        first, second = head_out(head), head_out(head + 1)
        o_ref[:, pair_of(head)] = jnp.where(lanes_like(first) < HEAD_DIM, first, second).astype(BF16)
    part_ref[...] = lax.dot_general(
        o_ref[...], w_ref[:, QKV_COLS:], NT, preferred_element_type=F32
    ).astype(BF16)

    at_grid(
        block,
        ends,
        steps_of(ring_g, 12.0),
        steps_of(ring_d, 12.0),
        timed([functools.partial(spread.forward, k) for k in range(CHUNKS)], 45, 48),
    )

    @pl.when(block == len(ends) - 1)
    def _():
        for item in (ring_g, ring_d, spread):
            item.finish()


def attend(count, a_all, w_attn, gain_q, gain_k, cosine, sine, bias, dy, shard_g, shard_d):
    seq, width = a_all.shape
    blocks = seq // Q_ROWS
    tall = GROUP * Q_ROWS
    shape = jax.ShapeDtypeStruct

    def rows(cols):
        return pl.BlockSpec((Q_ROWS, cols), lambda i: (i, 0))

    return pl.pallas_call(
        functools.partial(attend_kernel, count, blocks),
        grid=(blocks,),
        in_specs=[
            rows(width), one_buffer(w_attn.shape), one_buffer((1, 128)), one_buffer((1, 128)),
            rows(128), rows(128), one_buffer((1, seq)), HBM, HBM, HBM,
        ],
        out_specs=[
            rows(width), rows(Q_COLS), rows(128), rows(128), rows(QK_COLS), rows(Q_COLS),
            pl.BlockSpec((8, Q_ROWS), lambda i: (0, i)), HBM, HBM, HBM,
        ],
        out_shape=[
            shape((seq, width), BF16),
            shape((seq, Q_COLS), BF16),
            shape((seq, 128), BF16),
            shape((seq, 128), BF16),
            shape((seq, QK_COLS), F32),
            shape((seq, Q_COLS), BF16),
            shape((8, seq), F32),
            shape((4,) + dy.shape, BF16),
            shape((count,) + shard_g.shape, BF16),
            shape((count,) + shard_d.shape, BF16),
        ],
        scratch_shapes=[
            pltpu.VMEM((GROUPS, seq, 128), BF16),
            pltpu.VMEM((GROUPS, seq, 128), BF16),
            pltpu.VMEM((tall, seq), F32),
            pltpu.VMEM((tall, 128), F32),
            pltpu.VMEM((tall, 128), F32),
            pltpu.VMEM((GROUPS, tall, 128), F32),
        ]
        + RingGather.scratch(count, shard_g.shape[0])
        + RingGather.scratch(count, shard_d.shape[0])
        + Spread.scratch(),
        compiler_params=comm_params(5),
        name="attend",
    )(a_all, w_attn, gain_q, gain_k, cosine, sine, bias, dy, shard_g, shard_d)


B_ROWS = 512


def causal_pair(at, blocks):
    key_block, start, cum = 0, 0, 0
    for i in range(blocks - 1):
        cum += blocks - i
        past = (at >= cum).astype(jnp.int32)
        key_block = key_block + past
        start = start + past * (blocks - i)
    return key_block, at - start + key_block


def attend_back_kernel(
    count, blocks, q_ref, k_ref, v_ref, raw_ref, o_ref, lse_ref, dz_ref, a_ref, w_ref, gq_ref, gk_ref,
    cos_ref, sin_ref, bias_ref, pick_ref, grads, ffn_part, h_ref,
    part_ref, dw_ref, dgq_ref, dgk_ref, sum_g, sum_u, y_ref,
    do_scr, delta_scr, dq_scr, dk_scr, dv_scr, kd_scr, vd_scr, dwa_scr, dwo_scr, *scratch
):
    rows = k_ref.shape[0]
    now = pl.program_id(0)
    key_block, query_block = causal_pair(now, blocks)
    ring_g = RingScatter(
        count, lambda b, start, size: grads.at[0, b, pl.ds(start, size)], sum_g, *scratch[0:4]
    )
    ring_u = RingScatter(
        count, lambda b, start, size: grads.at[1, b, pl.ds(start, size)], sum_u, *scratch[4:8]
    )
    exchange = Exchange(ffn_part, *scratch[8:14])

    @pl.when(now == 0)
    def _():
        greet(tensor_peers() + ring_neighbours(count))
        exchange.begin()
        ring_g.begin()
        ring_u.begin()
        dq_scr[...] = jnp.zeros_like(dq_scr)
        dgq_ref[...] = jnp.zeros_like(dgq_ref)
        dgk_ref[...] = jnp.zeros_like(dgk_ref)
        dwa_scr[...] = jnp.zeros_like(dwa_scr)
        dwo_scr[...] = jnp.zeros_like(dwo_scr)

    at = pl.multiple_of(query_block * rows, rows)

    @pl.when(key_block == 0)
    def _():
        grad = jnp.dot(dz_ref[...], w_ref[:, QKV_COLS:], preferred_element_type=F32).astype(BF16)
        do_scr[pl.ds(at, rows), :] = grad
        delta_scr[:, pl.ds(at, rows)] = lax.dot_general(
            pick_ref[...], grad.astype(F32) * o_ref[...].astype(F32), NT,
            preferred_element_type=F32, precision=PRECISE,
        )
        dwo_scr[...] += lax.dot_general(dz_ref[...], o_ref[...], TN, preferred_element_type=F32)

    @pl.when(query_block == key_block)
    def _():
        for source, target in ((k_ref, kd_scr), (v_ref, vd_scr)):
            for group, one in enumerate(twice(source[...].astype(F32))):
                target[group] = one.astype(BF16)
        dk_scr[...] = jnp.zeros_like(dk_scr)
        dv_scr[...] = jnp.zeros_like(dv_scr)

    bias = bias_ref[...]

    def one(head, diagonal):
        group = head // GROUP
        query = only(head, q_ref[:, pair_of(head)])
        grad = only(head, do_scr[pl.ds(at, rows), pair_of(head)])
        score = lax.dot_general(kd_scr[group], query, NT, preferred_element_type=F32) + bias
        if diagonal:
            key_pos = lax.broadcasted_iota(jnp.int32, (rows, rows), 0)
            row_pos = lax.broadcasted_iota(jnp.int32, (rows, rows), 1)
            score = jnp.where(key_pos <= row_pos, score, MASKED_SCORE)
        prob = jnp.exp(score - lse_ref[head : head + 1, pl.ds(at, rows)])
        dv_scr[group] += jnp.dot(prob.astype(BF16), grad, preferred_element_type=F32)
        grad_prob = lax.dot_general(vd_scr[group], grad, NT, preferred_element_type=F32)
        grad_score = (prob * (grad_prob - delta_scr[head : head + 1, pl.ds(at, rows)])).astype(BF16)
        dk_scr[group] += jnp.dot(grad_score, query, preferred_element_type=F32)
        dq_scr[pl.ds(at, rows), pair_of(head)] += lax.dot_general(
            grad_score, only(head, kd_scr[group]), TN, preferred_element_type=F32
        )

    @pl.when(query_block == key_block)
    def _():
        for head in range(HEADS):
            one(head, True)

    @pl.when(query_block != key_block)
    def _():
        for head in range(HEADS):
            one(head, False)

    @pl.when(query_block == blocks - 1)
    def _():
        cosine, sine = cos_ref[...], sin_ref[...]

        def back(grad, raw, gain_ref, out_ref):
            grad = grad * cosine - turned(grad) * sine
            inverse = pair_inverse(raw)
            scaled = raw * inverse
            out_ref[...] += jnp.sum(grad * scaled, axis=0, keepdims=True)
            grad = grad * gain_ref[...]
            inner = both_sums(grad * scaled) * (1.0 / HEAD_DIM)
            return (inverse * (grad - scaled * inner)).astype(BF16)

        def joined(halves):
            total = [half + pltpu.roll(half, HEAD_DIM, 1) for half in (halves[0], halves[1])]
            return jnp.where(lanes_like(total[0]) < HEAD_DIM, total[0], total[1])

        mine = pl.ds(pl.multiple_of(key_block * rows, rows), rows)
        grads_qkv = [
            back(
                dq_scr[mine, pair_of(head)] * HEAD_DIM ** (-0.5),
                raw_ref[:, pair_of(head)], gq_ref, dgq_ref,
            )
            for head in range(0, HEADS, 2)
        ]
        grads_qkv.append(back(joined(dk_scr), raw_ref[:, Q_COLS:], gk_ref, dgk_ref))
        grads_qkv.append(joined(dv_scr).astype(BF16))
        grad_qkv = jnp.concatenate(grads_qkv, axis=1)
        part_ref[...] = lax.dot_general(
            grad_qkv, w_ref[:, :QKV_COLS], NT, preferred_element_type=F32
        ).astype(BF16)
        dwa_scr[...] += lax.dot_general(a_ref[...], grad_qkv, TN, preferred_element_type=F32)

    def land(k):
        lines = exchange.rows(k)
        y_ref[lines] = (h_ref[lines] + exchange.result(k)).astype(BF16)

    def each(call):
        return [functools.partial(call, k) for k in range(CHUNKS)]

    costs = []
    for i in range(blocks):
        for j in range(i, blocks):
            costs.append(5.4 + (3.5 if i == 0 else 0.0) + (5.0 if j == blocks - 1 else 0.0))
    ends = [sum(costs[: i + 1]) for i in range(len(costs))]
    at_grid(
        now,
        ends,
        timed(each(exchange.forward), 3, 3),
        timed(each(land), 40, 44),
        steps_of(ring_g, 12.0),
        steps_of(ring_u, 12.0),
    )

    @pl.when(now == len(ends) - 1)
    def _():
        dw_ref[:, :QKV_COLS] = dwa_scr[...].astype(BF16)
        dw_ref[:, QKV_COLS:] = dwo_scr[...].astype(BF16)
        for item in (ring_g, ring_u, exchange):
            item.finish()


def attend_back(
    count, query, key, value, raw, attn, lse, dz_all, a_all, w_attn, gain_q, gain_k, cosine, sine,
    bias_col, grads, up_rows, ffn_part, h
):
    seq, width = a_all.shape
    blocks = seq // B_ROWS
    _, _, own, cols = grads.shape
    shape = jax.ShapeDtypeStruct
    pick = (jnp.arange(8)[:, None] == jnp.arange(Q_COLS)[None, :] // HEAD_DIM).astype(F32)

    def by_key(wide):
        return pl.BlockSpec((B_ROWS, wide), lambda i: (causal_pair(i, blocks)[0], 0))

    def by_query(wide):
        return pl.BlockSpec((B_ROWS, wide), lambda i: (causal_pair(i, blocks)[1], 0))

    def at_first(wide):
        return pl.BlockSpec((B_ROWS, wide), lambda i: (jnp.minimum(i, blocks - 1), 0))

    return pl.pallas_call(
        functools.partial(attend_back_kernel, count, blocks),
        grid=(blocks * (blocks + 1) // 2,),
        in_specs=[
            by_query(Q_COLS), by_key(128), by_key(128), by_key(QK_COLS), at_first(Q_COLS),
            one_buffer((8, seq)), at_first(width), by_key(width), one_buffer(w_attn.shape),
            one_buffer((1, 128)), one_buffer((1, 128)), by_key(128), by_key(128), by_key(1),
            one_buffer((8, Q_COLS)), HBM, HBM, one_buffer(h.shape),
        ],
        out_specs=[
            by_key(width), one_buffer(w_attn.shape), one_buffer((1, 128)), one_buffer((1, 128)),
            one_buffer((own, cols)), one_buffer((up_rows, cols)), one_buffer(h.shape),
        ],
        out_shape=[
            shape((seq, width), BF16),
            shape(w_attn.shape, BF16),
            shape((1, 128), F32),
            shape((1, 128), F32),
            shape((own, cols), F32),
            shape((up_rows, cols), F32),
            shape(h.shape, BF16),
        ],
        scratch_shapes=[
            pltpu.VMEM((seq, Q_COLS), BF16),
            pltpu.VMEM((8, seq), F32),
            pltpu.VMEM((seq, Q_COLS), F32),
            pltpu.VMEM((GROUPS, B_ROWS, 128), F32),
            pltpu.VMEM((GROUPS, B_ROWS, 128), F32),
            pltpu.VMEM((GROUPS, B_ROWS, 128), BF16),
            pltpu.VMEM((GROUPS, B_ROWS, 128), BF16),
            pltpu.VMEM((width, QKV_COLS), F32),
            pltpu.VMEM((width, Q_COLS), F32),
        ]
        + RingScatter.scratch(count, own, cols)
        + RingScatter.scratch(count, up_rows, cols)
        + Exchange.scratch(*h.shape),
        compiler_params=comm_params(6),
        name="attend_back",
    )(
        query, key, value, raw, attn, lse, dz_all, a_all, w_attn, gain_q, gain_k, cosine, sine,
        bias_col, pick, grads, ffn_part, h,
    )


PRE_COLS = 512


def precondition_kernel(
    total_cols, p_ref, w_ref, f_ref, s_ref, l_ref, lt_ref, r_ref, ls_ref, lf_ref,
    wo_ref, fo_ref, so_ref, rso_ref, lso_ref, at_ref,
):
    rows, width = p_ref.shape
    step = pl.program_id(0)
    valid = (
        step * width + lax.broadcasted_iota(jnp.int32, (rows, width), 1) < total_cols
    )
    grad = jnp.where(valid, p_ref[...], 0.0)
    low = grad.astype(BF16)
    half = jnp.dot(lt_ref[...], low, preferred_element_type=F32).astype(BF16)
    pairs = width // 128
    turned = jnp.concatenate(
        [
            jnp.dot(half[:, i * 128 : (i + 1) * 128], r_ref[i], preferred_element_type=F32)
            for i in range(pairs)
        ],
        axis=1,
    )
    first = MOMENT_DECAY * f_ref[...] + (1.0 - MOMENT_DECAY) * turned
    second = MOMENT_DECAY * s_ref[...] + (1.0 - MOMENT_DECAY) * turned * turned
    fo_ref[...] = first
    so_ref[...] = second
    correction = 1.0 - MOMENT_DECAY**STEP
    direction = first / correction / (jnp.sqrt(second / correction) + ADAM_EPSILON)
    direction = jnp.where(valid, direction, 0.0).astype(BF16)
    back = jnp.dot(l_ref[...], direction, preferred_element_type=F32).astype(BF16)
    update = jnp.concatenate(
        [
            lax.dot_general(
                back[:, i * 128 : (i + 1) * 128], r_ref[i], NT, preferred_element_type=F32
            )
            for i in range(pairs)
        ],
        axis=1,
    )
    weight = w_ref[...]
    wo_ref[...] = weight - RATE_WEIGHT * (update + DECAY_WEIGHT * weight)
    for i in range(pairs):
        tile = low[:, i * 128 : (i + 1) * 128]
        cov = lax.dot_general(tile, tile, TN, preferred_element_type=F32)
        for j in range(2):
            rso_ref[2 * i + j] = cov[j * 64 : (j + 1) * 64, j * 64 : (j + 1) * 64]

    @pl.when(step == 0)
    def _():
        lso_ref[...] = MOMENT_DECAY * ls_ref[...]

    lso_ref[...] += (1.0 - MOMENT_DECAY) * lax.dot_general(
        low, low, NT, preferred_element_type=F32
    )

    @pl.when(step == pl.num_programs(0) - 1)
    def _():
        at_ref[...] = lax.dot_general(
            lf_ref[...], lso_ref[...], NT, preferred_element_type=F32, precision=PRECISE
        )


def precondition(grad, weight, first, second, left, pairs, tiles, left_stat):
    rows, cols = grad.shape
    per = PRE_COLS // 64
    flat = pl.BlockSpec((rows, PRE_COLS), lambda i: (0, i))
    deep = pl.BlockSpec((rows, None, PRE_COLS), lambda i: (0, 0, i))
    square = pl.BlockSpec((rows, rows), lambda i: (0, 0))
    right = pl.BlockSpec((per, 64, 64), lambda i: (i, 0, 0))
    left_t = left.T
    return pl.pallas_call(
        functools.partial(precondition_kernel, cols),
        grid=(pl.cdiv(cols, PRE_COLS),),
        in_specs=[
            flat, deep, deep, deep, square, square,
            pl.BlockSpec((per // 2, 128, 128), lambda i: (i, 0, 0)),
            square, square,
        ],
        out_specs=[deep, deep, deep, right, square, square],
        out_shape=[
            jax.ShapeDtypeStruct((rows, 1, cols), F32),
            jax.ShapeDtypeStruct((rows, 1, cols), F32),
            jax.ShapeDtypeStruct((rows, 1, cols), F32),
            jax.ShapeDtypeStruct((tiles, 64, 64), F32),
            jax.ShapeDtypeStruct((rows, rows), F32),
            jax.ShapeDtypeStruct((rows, rows), F32),
        ],
        compiler_params=params("arbitrary"),
        cost_estimate=pl.CostEstimate(
            flops=rows * cols * 2 * 1500, bytes_accessed=rows * cols * 28, transcendentals=rows * cols
        ),
        name="precondition",
    )(grad, weight, first, second, left.astype(BF16), left_t.astype(BF16), pairs, left_stat, left_t)


def right_basis_kernel(cov_ref, old_ref, r_ref, stat_ref, q_ref, norm_ref):
    size = r_ref.shape[0]
    lanes = r_ref.shape[2]
    unroll = 8
    pair = 2

    def start(step, s):
        at = step * pair
        rows = []
        for j in range(pair):
            stat = MOMENT_DECAY * old_ref[at + j] + (1.0 - MOMENT_DECAY) * cov_ref[at + j]
            stat_ref[at + j] = stat
            rows.append(stat)
        sums = [row[0:1] * r_ref[0] for row in rows]
        for k in range(1, size):
            right = r_ref[k]
            sums = [total + row[k : k + 1] * right for total, row in zip(sums, rows)]
        for j in range(pair):
            q_ref[at + j] = sums[j]
            s = s + sums[j] * sums[j][0:1]
        return s

    s = lax.fori_loop(0, size // pair, start, jnp.zeros((size, lanes), F32))
    for k in range(size):
        low = (k // 8) * 8
        nxt = min(((k + 1) // 8) * 8, size - 8)
        squared = s[k - low : k - low + 1]
        norm_ref[k : k + 1] = lax.rsqrt(squared)
        if k == size - 1:
            break
        ids = low + lax.broadcasted_iota(jnp.int32, s.shape, 0)
        coef = jnp.where(ids > k, s / squared, 0.0)

        def update(i, s_next, k=k, low=low, nxt=nxt, coef=coef):
            row = q_ref[i, low:size, :]
            new = row - row[k - low : k - low + 1] * coef
            q_ref[i, low:size, :] = new
            new = new[nxt - low :]
            return s_next + new * new[k + 1 - nxt : k + 2 - nxt]

        s = lax.fori_loop(
            0, size, update, jnp.zeros((size - nxt, s.shape[1]), F32), unroll=unroll
        )
    norms = norm_ref[...]

    def finish(i, carry):
        q_ref[i] = q_ref[i] * norms
        return carry

    lax.fori_loop(0, size, finish, 0, unroll=unroll)


def right_orthonormal(cov, old, right):
    size, _, count = right.shape
    shape = jax.ShapeDtypeStruct(right.shape, F32)
    return pl.pallas_call(
        right_basis_kernel,
        out_shape=[shape, shape],
        scratch_shapes=[pltpu.VMEM((size, count), F32)],
        compiler_params=params(),
        cost_estimate=pl.CostEstimate(
            flops=4 * size**3 * count * 16, bytes_accessed=20 * size * size * 128, transcendentals=0
        ),
        name="right_orthonormal",
    )(cov, old, right)


def left_basis_kernel(panel, a_ref, q_ref):
    rows, width = a_ref.shape
    q_ref[...] = a_ref[...]
    for start in range(0, rows, panel):
        ids = lax.broadcasted_iota(jnp.int32, (panel, 1), 0)

        def step(k, carry, start=start, ids=ids):
            line = q_ref[pl.ds(start + k, 1), :]
            block = q_ref[start : start + panel, :]
            squared = jnp.sum(line * line, axis=1, keepdims=True)
            inner = jnp.sum(block * line, axis=1, keepdims=True)
            coef = jnp.where(ids > k, inner / squared, 0.0)
            q_ref[start : start + panel, :] = block - coef * line
            return carry

        lax.fori_loop(0, panel, step, 0)
        block = q_ref[start : start + panel, :]
        block = block * lax.rsqrt(jnp.sum(block * block, axis=1, keepdims=True))
        q_ref[start : start + panel, :] = block
        if start + panel < rows:
            rest = q_ref[start + panel :, :]
            inner = lax.dot_general(rest, block, NT, preferred_element_type=F32, precision=PRECISE)
            q_ref[start + panel :, :] = rest - jnp.dot(
                inner, block, preferred_element_type=F32, precision=PRECISE
            )


def left_orthonormal(matrix_t):
    rows = matrix_t.shape[0]
    panel = 64 if rows % 64 == 0 else rows
    return pl.pallas_call(
        functools.partial(left_basis_kernel, panel),
        out_shape=jax.ShapeDtypeStruct(matrix_t.shape, F32),
        compiler_params=params(),
        cost_estimate=pl.CostEstimate(
            flops=rows**3 * 200, bytes_accessed=8 * rows * rows, transcendentals=0
        ),
        name="left_orthonormal",
    )(matrix_t)


def sum_everywhere(vector):
    for axis in ("tensor", "dp"):
        count = lax.axis_size(axis)
        bit = 1
        while bit < count:
            vector = vector + lax.ppermute(vector, axis, [(i, i ^ bit) for i in range(count)])
            bit *= 2
    return vector


def mul(left, right, dims=(((1,), (0,)), ((), ())), out=F32):
    return lax.dot_general(left, right, dims, preferred_element_type=F32).astype(out)


def body(
    layer_input, cotangent, lengths, owners, weight, weight_first, weight_second,
    left_basis, right_basis, left_stat, right_stat, norm_gains, gain_first, gain_second,
):
    tensor_total = lax.axis_size("tensor")
    count = lax.axis_size("dp")
    rows_here, slots_here, model_width = layer_input.shape
    assert tensor_total == 4 and slots_here == 1
    seq_all = rows_here * tensor_total
    own_rows, _, cols_all = weight.shape
    query_cols = QUERY_HEADS * HEAD_DIM // tensor_total
    kv_cols = KEY_VALUE_HEADS * HEAD_DIM // tensor_total
    ff_cols = FF // tensor_total
    off_gate = query_cols + 2 * kv_cols
    off_out = off_gate + 2 * ff_cols
    off_down = off_out + query_cols

    ids = jnp.arange(count, dtype=jnp.int32)
    holds = jnp.sum(jnp.where(owners[None, :] == ids[:, None], ids[None, :], 0), axis=1)
    true_column = (holds[:, None] * own_rows + jnp.arange(own_rows, dtype=jnp.int32)[None, :]).reshape(-1)
    move = (jnp.arange(model_width, dtype=jnp.int32)[:, None] == true_column[None, :]).astype(BF16)

    def held_gain(vector):
        return jnp.take(vector.reshape(count, own_rows), holds, axis=0).reshape(1, model_width)

    def true_gain(vector):
        return jnp.take(vector.reshape(count, own_rows), owners, axis=0).reshape(-1)

    weight2 = weight.reshape(own_rows, cols_all)
    low_w = weight2.astype(BF16)
    shard_attn = jnp.concatenate([low_w[:, :off_gate], low_w[:, off_out:off_down]], axis=1)
    shard_gate = low_w[:, off_gate : off_gate + ff_cols]
    shard_up = low_w[:, off_gate + ff_cols : off_out]
    shard_down = low_w[:, off_down:]

    gain_in = held_gain(norm_gains[:MODEL_DIM])
    gain_mid = held_gain(norm_gains[MODEL_DIM : 2 * MODEL_DIM])
    gain_query = norm_gains[2 * MODEL_DIM : 2 * MODEL_DIM + HEAD_DIM]
    gain_key = norm_gains[2 * MODEL_DIM + HEAD_DIM :]
    cosine, sine = lane_tables(seq_all)
    rank = lax.axis_index("tensor")
    positions = rank * rows_here + jnp.arange(rows_here, dtype=jnp.int32)
    live = (positions < lengths[0]).astype(BF16)[:, None]
    x_low = mul(layer_input.reshape(rows_here, model_width), move, out=BF16)
    grad_low = mul(cotangent.reshape(rows_here, model_width) * live, move, out=BF16)
    normed_in = rms_rows(x_low.astype(F32), gain_in)[0].astype(BF16)
    low_in, w_attn = front(count, normed_in, shard_attn)
    low_in = low_in.reshape(seq_all, model_width)
    w_attn = w_attn.reshape(model_width, off_gate + query_cols)
    half_rows = 16 * (own_rows // 32)
    gain_query = jnp.tile(gain_query, 2)[None, :]
    gain_key = jnp.tile(gain_key, 2)[None, :]
    bias = jnp.where(jnp.arange(seq_all, dtype=jnp.int32) < lengths[0], 0.0, MASKED_SCORE).astype(F32)
    attn_part, query, key, value, raw, attn, lse, grad_out_all, w_gate, w_down_a = attend(
        count, low_in, w_attn, gain_query, gain_key, cosine, sine, bias[None, :],
        grad_low, shard_gate, shard_down[:half_rows],
    )
    grad_out_all = grad_out_all.reshape(seq_all, model_width)
    w_gate = w_gate.reshape(model_width, ff_cols)

    ranked = (tensor_total, rows_here, model_width)
    blocked = (count, own_rows)
    attn_part = attn_part.reshape(ranked)
    resid_mid, low_mid, w_up, w_down_b = middle(
        count, attn_part, x_low, gain_mid, shard_up, shard_down[half_rows:]
    )
    low_mid = low_mid.reshape(seq_all, model_width)
    w_up = w_up.reshape(model_width, ff_cols)
    w_down = jnp.concatenate([w_down_a, w_down_b], axis=1).reshape(model_width, ff_cols)

    hidden3, grad_mid_part = feed_forward(low_mid, grad_out_all, w_gate, w_up, w_down)
    d_gu, ffn_part, grad_resid, gain_mid_grad, grad_resid_all, sum_down = turn(
        count, grad_mid_part.reshape(ranked), resid_mid, grad_low, gain_mid,
        grad_out_all, low_mid, hidden3, w_down,
    )
    ffn_part = ffn_part.reshape(ranked)
    d_gu = d_gu.reshape((2,) + blocked + (ff_cols,))

    grad_in_part, d_attn, gain_query_grad, gain_key_grad, sum_gate, sum_up_a, out_held = attend_back(
        count, query, key, value, raw, attn, lse, grad_resid_all.reshape(seq_all, model_width), low_in,
        w_attn, gain_query, gain_key, cosine, sine, bias[:, None], d_gu, half_rows, ffn_part, resid_mid,
    )
    layer_output = mul(out_held, move, NT, BF16)
    d_attn = d_attn.reshape(blocked + (off_gate + query_cols,))
    grad_in_part = grad_in_part.reshape(ranked)
    gain_query_grad = jnp.sum(gain_query_grad.reshape(2, HEAD_DIM), axis=0)
    gain_key_grad = jnp.sum(gain_key_grad.reshape(2, HEAD_DIM), axis=0)
    grad_held, gain_in_grad, sum_up_b, sum_attn = last(
        count, grad_in_part, x_low, grad_resid, gain_in, d_gu, half_rows, d_attn
    )
    sum_up = jnp.concatenate([sum_up_a, sum_up_b], axis=0)
    grad_top = grad_held.astype(BF16)
    grad_rest = (grad_held - grad_top.astype(F32)).astype(BF16)
    input_grad = mul(grad_top, move, NT) + mul(grad_rest, move, NT)

    gain_grad = sum_everywhere(
        jnp.concatenate(
            [true_gain(gain_in_grad), true_gain(gain_mid_grad), gain_query_grad, gain_key_grad]
        )
    )
    moment_one = MOMENT_DECAY * gain_first + (1.0 - MOMENT_DECAY) * gain_grad
    moment_two = MOMENT_DECAY * gain_second + (1.0 - MOMENT_DECAY) * gain_grad * gain_grad
    correction = 1.0 - MOMENT_DECAY**STEP
    gains_new = norm_gains - RATE_GAIN * (moment_one / correction) / (
        jnp.sqrt(moment_two / correction) + ADAM_EPSILON
    )

    grad_own = jnp.concatenate(
        [sum_attn[:, :off_gate], sum_gate, sum_up, sum_attn[:, off_gate:], sum_down], axis=1
    )
    tiles = cols_all // 64
    right = right_basis.reshape(tiles, 64, 64)
    even = jnp.pad(right, ((0, tiles % 2), (0, 0), (0, 0))).astype(BF16).reshape(-1, 2, 64, 64)
    pairs = jnp.concatenate(
        [
            jnp.pad(even[:, 0], ((0, 0), (0, 0), (0, 64))),
            jnp.pad(even[:, 1], ((0, 0), (0, 0), (64, 0))),
        ],
        axis=1,
    )
    weight_new, first_new, second_new, right_cov, left_stat_new, left_a_t = precondition(
        grad_own,
        weight,
        weight_first,
        weight_second,
        left_basis.reshape(own_rows, own_rows),
        pairs,
        tiles,
        left_stat.reshape(own_rows, own_rows),
    )
    left_new = left_orthonormal(left_a_t).T
    right_stat_new, right_new = right_orthonormal(
        right_cov.transpose(1, 2, 0),
        right_stat.reshape(tiles, 64, 64).transpose(1, 2, 0),
        right.transpose(1, 2, 0),
    )
    right_stat_new = right_stat_new.transpose(2, 0, 1)
    right_new = right_new.transpose(2, 0, 1)
    return (
        layer_output.reshape(layer_input.shape),
        input_grad.reshape(layer_input.shape),
        weight_new.reshape(weight.shape),
        first_new.reshape(weight.shape),
        second_new.reshape(weight.shape),
        left_new.reshape(left_basis.shape),
        right_new.reshape(right_basis.shape),
        left_stat_new.reshape(left_stat.shape),
        right_stat_new.reshape(right_stat.shape),
        moment_one,
        moment_two,
        gains_new,
    )


def solution(mesh):
    whole, flat = P(), P("dp", "tensor", None)
    rows, tiles = P("tensor", "dp", None), P("dp", "tensor", None, None, None)
    in_specs = (
        rows, rows, P("dp"), whole, flat, flat, flat, flat, tiles, flat, tiles, whole, whole, whole,
    )
    out_specs = (rows, rows, flat, flat, flat, flat, tiles, flat, tiles, whole, whole, whole)
    return jax.shard_map(body, mesh=mesh, in_specs=in_specs, out_specs=out_specs, check_vma=False)
```

time: 3630 us -> 756 us (0.21)
  waiting for transfers between devices: 1820 us -> 0.01 us
  other arithmetic: 950 us -> 28 us
  Pallas kernels: 0 us -> 659 us
  matrix products: 488 us -> 20.3 us
  local copies, waits for them, and re-layouts: 297 us -> 38.2 us
  blocking collectives: 43.5 us -> 0 us
    unnamed x11 -> x0, waiting for transfers between devices: 1080 us -> none
    another operation x22 -> x1, other arithmetic: 696 us -> 0.2 us  [the longest x11 601 us: orthonormal(): factor = jnp.linalg.cholesky(gram_matrix)]
    pallas_call x0 -> x10, Pallas kernels: none -> 659 us  [the longest x1 106 us: attend_back(): pl.pallas_call(functools.partial(attend_back_kernel, count, blocks), grid...]
    all_gather x5 -> x0, waiting for transfers between devices: 469 us -> none  [the longest x1 362 us: body(): joined_w = arrange(lax.all_gather(weight_low, 'dp', axis=0, tiled=True))]
    dot_general x46 -> x5, matrix products: 478 us -> 20.3 us  [mul(): lax.dot_general(left, right, dims, preferred_element_type=F32).astype(out)]
    reduce_scatter x4 -> x0, waiting for transfers between devices: 278 us -> none  [the longest x2 197 us: branch_sum(): lax.psum_scatter(jnp.einsum('tsc,dc->tsd', left_rows, right_w, preferred_...]
    gather x8 -> x4, local copies, waits for them, and re-layouts: 94.8 us -> 2.25 us  [the longest x2 1.12 us: true_gain(): return jnp.take(vector.reshape(count, own_rows), owners, axis=0).reshape(-1)]
    convert_element_type x9 -> x4, other arithmetic: 78.4 us -> 2.87 us  [the longest x1 1.57 us: body(): normed_in = rms_rows(x_low.astype(F32), gain_in)[0].astype(BF16)]
  transfers between devices with their start and end apart: 10 -> 5, of which waited for: 8 -> 0; matrix products, arithmetic and copies ran while one was open for 11% -> 5% of each run, Pallas kernels for 0% -> 10%
where the time goes in v1:
time: 756 us; the launch traced here: 752 us
  Pallas kernels  659 us (87%)
  local copies, waits for them, and re-layouts  38.2 us (5%)
  other arithmetic  28 us (4%)
  matrix products  20.3 us (3%)
    pallas_call x1, Pallas kernels, attend_back(): pl.pallas_call(functools.partial(attend_back_kernel, count, blocks), grid...  106 us
    pallas_call x1, Pallas kernels, turn(): pl.pallas_call(functools.partial(turn_kernel, count, own, ff_steps), grid...  95.5 us
    pallas_call x1, Pallas kernels, attend(): pl.pallas_call(functools.partial(attend_kernel, count, blocks), grid=(blo...  88.2 us
    pallas_call x1, Pallas kernels, middle(): pl.pallas_call(functools.partial(middle_kernel, count), in_specs=[HBM, vm...  85.5 us
    pallas_call x1, Pallas kernels, feed_forward(): pl.pallas_call(feed_forward_kernel, grid=(seq // FF_ROWS,), in_specs=[row...  76.5 us
    pallas_call x1, Pallas kernels, last(): pl.pallas_call(functools.partial(last_kernel, count, first), in_specs=[HB...  65 us
    pallas_call x1, Pallas kernels, front(): pl.pallas_call(functools.partial(front_kernel, count), in_specs=[HBM] * 2...  64.4 us
    pallas_call x1, Pallas kernels, right_orthonormal(): pl.pallas_call(right_basis_kernel, out_shape=[shape, shape], scratch_shap...  30 us
  transfers between devices with their start and end apart: 5, of which 0 were waited for; matrix products, arithmetic and copies ran while one was open for 5% of the time, Pallas kernels for 10%

profile of v1, /device:TPU:0, one launch (start us, length us, event | category | flops | bytes accessed | tf_op | source)
XLA Modules:
  0.0 751.8 jit_solution(11840190023526738506)
XLA Ops:
  0.7 0.9 select_reduce_fusion
  1.6 2.6 copy.67
  4.3 0.6 fusion.42
  4.9 0.5 negate_power_fusion
  5.4 1.3 fusion.40
  6.7 0.9 fusion.39
  7.7 0.6 add_select_fusion
  8.4 0.6 gather_fusion.1
  9.0 0.6 gather_fusion
  9.7 0.7 reshape.260.g_ref
  10.3 0.6 compare_select_fusion.1
  10.9 0.5 compare_and_fusion
  11.5 0.7 add.89
  12.2 3.7 fusion.14
  15.9 0.8 broadcast_in_dim_tile.6.gq_ref
  16.7 0.7 tile.5
  17.4 0.7 broadcast_in_dim_tile.7.gk_ref
  18.0 5.6 fusion.31
  24.3 0.6 compare_select_fusion.bias_ref
  24.9 0.7 reshape.249.g_ref
  25.6 1.1 fusion.27.bias_ref
  26.7 0.6 fusion.33.pick_ref
  27.3 0.8 pad_maximum_fusion.4.wa_ref
  28.1 1.6 fusion.16.a_ref
  29.6 64.4 %front.1 = (bf16[4,512,1536]{2,1,0:T(8,128)(2,1)}, bf16[8,192,1024]{2,1,0:T(8,128)(2,1)}) custom-call(bf16[512,1536]{1,0:T(8,128)(2,1)} %fusion.16.a_ref, bf16[192,1024]{1,0:T(8,128)(2,1)} %pad_maximum_fusion.4.wa_ref), custom_call_target="tpu_custom_call" | custom-call | tf_op jit(solution)/shard_map/front/pallas_call | solution.py:471
  94.1 5.4 fusion.18.dy_ref
  99.6 3.0 pad_maximum_fusion.2
  102.6 88.2 %attend.1 = (bf16[2048,1536]{1,0:T(8,128)(2,1)}, bf16[2048,384]{1,0:T(8,128)(2,1)}, bf16[2048,128]{1,0:T(8,128)(2,1)}, bf16[2048,128]{1,0:T(8,128)(2,1)}, f32[20...) custom-call(bf16[2048,1536]{1,0:T(8,128)(2,1)} %bitcast.73, ...), custom_call_target="tpu_custom_call" | custom-call | tf_op jit(solution)/shard_map/attend/pallas_call | solution.py:932
  190.8 85.5 %middle.1 = (f32[512,1536]{1,0:T(8,128)}, bf16[4,512,1536]{2,1,0:T(8,128)(2,1)}, bf16[8,192,1728]{2,1,0:T(8,128)(2,1)}, bf16[8,96,1728]{2,1,0:T(8,128)(2,1)}) custom-call(bf16[4,512,1536]{2,1,0:T(8,128)(2,1)} %bitcast.88, bf16[512,1536]{1,0:T(8,128)(2,1)} %copy-done.2, f32[1,1536]{1,0:T(1,128)} %reshape.249.g_ref, ...), custom_call_target="tpu_custom_call" | custom-call | tf_op jit(solution)/shard_map/middle/pallas_call | solution.py:521
  276.4 4.6 pad_maximum_fusion
  281.0 76.5 %feed_forward.1 = (bf16[3,2048,1728]{2,1,0:T(8,128)(2,1)}, bf16[2048,1536]{1,0:T(8,128)(2,1)}) custom-call(bf16[2048,1536]{1,0:T(8,128)(2,1)} %bitcast.92, bf16[2048,1536]{1,0:T(8,128)(2,1)} %bitcast.90, bf16[1536,1728]{1,0:T(8,128)(2,1)} %bitcast.101, bf16[1536,1728]{1,0:T(8,128)(2,1)} %bitcast.102, bf16[1536,1728]{1,0:T(8,128)(2,1)} %bitcast.75), custom_call_target="tpu_custom_call" | custom-call | flops 54358179840 | bytes 53477376 | tf_op jit(solution)/shard_map/feed_forward/pallas_call | solution.py:574
  357.5 95.5 %turn.1 = (bf16[2,1536,1728]{2,1,0:T(8,128)(2,1)}, bf16[2048,1536]{1,0:T(8,128)(2,1)}, f32[512,1536]{1,0:T(8,128)}, f32[1,1536]{1,0:T(1,128)}, bf16[4,512,1536]{2,1,0:T(8,128)(2,1)}, /*index=5*/f32[192,1728]{1,0:T(8,128)}) custom-call(bf16[2048,1536]{1,0:T(8,128)(2,1)} %bitcast.91, bf16[2048,1536]{1,0:T(8,128)(2,1)} %bitcast.93, ...), custom_call_target="tpu_custom_call" | custom-call | tf_op jit(solution)/shard_map/turn/pallas_call | solution.py:686
  453.1 0.7 reduce.1
  453.9 106.1 %attend_back.1 = (bf16[2048,1536]{1,0:T(8,128)(2,1)}, bf16[1536,1024]{1,0:T(8,128)(2,1)}, f32[1,128]{1,0:T(1,128)}, f32[1,128]{1,0:T(1,128)}, f32[192,1728]{1,0:...) custom-call(bf16[2048,384]{1,0:T(8,128)(2,1)} %get-tuple-element.58.q_ref, ...), custom_call_target="tpu_custom_call" | custom-call | tf_op jit(solution)/shard_map/attend_back/pallas_call | solution.py:1144
  560.0 65.0 %last.1 = (f32[512,1536]{1,0:T(8,128)}, f32[1,1536]{1,0:T(1,128)}, f32[96,1728]{1,0:T(8,128)}, f32[192,1024]{1,0:T(8,128)}) custom-call(bf16[4,512,1536]{2,1,0:T(8,128)(2,1)} %bitcast.89, bf16[512,1536]{1,0:T(8,128)(2,1)} %copy-done.2, f32[512,1536]{1,0:T(8,128)} %get-tuple-element.79.d_ref, f32[1,1536]{1,0:T(1,128)} %reshape.260.g_ref, ...), custom_call_target="tpu_custom_call" | custom-call | tf_op jit(solution)/shard_map/last/pallas_call | solution.py:768
  625.1 0.7 reduce
  625.9 0.6 gather_fusion.3
  626.4 0.6 gather_fusion.2
  627.2 0.5 broadcast.221
  627.8 0.7 reduce.8
  628.5 0.7 reduce.9
  629.4 4.0 fusion.20
  633.4 2.7 fusion
  636.2 4.5 fusion.13
  641.0 2.6 copy.62
  644.3 0.5 copy-done.10
  645.1 0.7 bitcast_convert_fusion.2
  645.8 0.5 collective-permute-start.1
  646.3 1.6 fusion.23.r_ref
  648.0 1.6 copy.53.l_ref
  649.7 1.6 copy.68
  651.3 4.8 concatenate.29.p_ref
  656.1 0.7 add.96
  656.8 1.6 collective-permute-start.2
  658.4 25.3 %precondition.1 = (f32[192,1,6208]{2,1,0:T(1,128)}, f32[192,1,6208]{2,1,0:T(1,128)}, f32[192,1,6208]{2,1,0:T(1,128)}, f32[97,64,64]{2,1,0:T(8,128)}, f32[192,192]{1,0:T(8,128)}, /*index=5*/f32[192,192]{1,0:T(8,128)}) custom-call(f32[192,6208]{1,0:T(8,128)} %concatenate.29.p_ref, f32[192,1,6208]{2,1,0:T(1,128)} %w_ref.1, f32[192,1,6208]{2,1,0:T(1,128)} %f_ref.1, ...), custom_call_target="tpu_custom_call" | custom-call | flops 3575808000 | bytes 33374208 | tf_op jit(solution)/shard_map/precondition/pallas_call | solution.py:1259
  683.7 4.2 copy.54
  687.9 0.5 collective-permute-start.3
  688.4 30.0 %right_orthonormal.1 = (f32[64,64,97]{2,1,0:T(8,128)}, f32[64,64,97]{2,1,0:T(8,128)}) custom-call(f32[64,64,97]{2,1,0:T(8,128)} %bitcast.84, f32[64,64,97]{2,1,0:T(8,128)} %bitcast.96, f32[64,64,97]{2,1,0:T(8,128)} %bitcast.83), custom_call_target="tpu_custom_call" | custom-call | flops 1627389952 | bytes 10485760 | tf_op jit(solution)/shard_map/right_orthonormal/pallas_call | solution.py:1339
  718.5 1.5 collective-permute-start.4
  720.0 22.4 %left_orthonormal.1 = f32[192,192]{1,0:T(8,128)} custom-call(f32[192,192]{1,0:T(8,128)} %get-tuple-element.90.a_ref), custom_call_target="tpu_custom_call" | custom-call | flops 1415577600 | bytes 294912 | tf_op jit(solution)/shard_map/left_orthonormal/pallas_call | solution.py:1381
  742.4 6.8 copy.55
  749.2 0.8 copy.56
  750.0 0.9 copy.57
  750.9 0.6 divide_subtract_fusion
  (98 shorter events, 2.5 us)
Async XLA Ops:
  0.6 11.6 %copy-start = (bf16[512,1,1536]{2,0,1:T(8,128)(2,1)S(1)}, bf16[512,1,1536]{2,0,1:T(8,128)(2,1)}, u32[]{:S(2)}) copy-start(bf16[512,1,1536]{2,0,1:T(8,128)(2,1)} %param.16) | copy-start | bytes 4718596
  1.6 2.7 copy-start.15
  4.2 6.1 copy-start.26
  12.2 3.7 copy-start.23
  15.9 13.8 %copy-start.2 = (bf16[512,1536]{1,0:T(8,128)(2,1)}, bf16[512,1536]{1,0:T(8,128)(2,1)S(1)}, u32[]{:S(2)}) copy-start(bf16[512,1536]{1,0:T(8,128)(2,1)S(1)} %get-tuple-element.160.x_ref) | copy-start | bytes 4718596
  15.9 10.8 %copy-start.19 = (s32[384]{0:T(512)S(1)}, s32[384]{0:T(512)}, u32[]{:S(2)}) copy-start(s32[384]{0:T(512)} %add_select_fusion) | copy-start | bytes 4612
  26.7 67.4 %copy-start.20 = (s32[1536]{0:T(1024)S(1)}, s32[1536]{0:T(1024)}, u32[]{:S(2)}) copy-start(s32[1536]{0:T(1024)} %add.89) | copy-start | bytes 18436
  94.1 5.4 copy-start.4
  94.1 5.4 copy-start.5
  190.8 85.6 %copy-start.6 = (bf16[8,96,1728]{2,1,0:T(8,128)(2,1)S(1)}, bf16[8,96,1728]{2,1,0:T(8,128)(2,1)}, u32[]{:S(2)}) copy-start(bf16[8,96,1728]{2,1,0:T(8,128)(2,1)} %get-tuple-element.69) | copy-start | bytes 7962628
  357.5 96.4 %copy-start.22 = (s32[8]{0:T(128)S(1)}, s32[8]{0:T(128)}, u32[]{:S(2)}) copy-start(s32[8]{0:T(128)} %compare_select_fusion.1) | copy-start | bytes 100
  560.0 67.0 %copy-start.21 = (pred[8]{0:T(512)(128)(4,1)S(1)}, pred[8]{0:T(512)(128)(4,1)}, u32[]{:S(2)}) copy-start(pred[8]{0:T(512)(128)(4,1)} %compare_and_fusion) | copy-start | bytes 28
  560.0 67.8 %copy-start.28 = (f32[1,128]{1,0:T(1,128)S(1)}, f32[1,128]{1,0:T(1,128)}, u32[]{:S(2)}) copy-start(f32[1,128]{1,0:T(1,128)} %get-tuple-element.97) | copy-start | bytes 1540
  560.0 68.5 %copy-start.27 = (f32[1,128]{1,0:T(1,128)S(1)}, f32[1,128]{1,0:T(1,128)}, u32[]{:S(2)}) copy-start(f32[1,128]{1,0:T(1,128)} %get-tuple-element.98) | copy-start | bytes 1540
  560.0 69.4 %copy-start.25 = (bf16[512,1536]{1,0:T(8,128)(2,1)S(1)}, bf16[512,1536]{1,0:T(8,128)(2,1)}, u32[]{:S(2)}) copy-start(bf16[512,1536]{1,0:T(8,128)(2,1)} %get-tuple-element.77) | copy-start | bytes 4718596
  629.4 16.4 %collective-permute-start = (f32[3200]{0:T(1024)S(1)}, f32[3200]{0:T(1024)S(1)}, u32[]{:S(2)}, u32[]{:S(2)}) collective-permute-start(f32[3200]{0:T(1024)S(1)} %concatenate.31), channel_id=1, source_target_pairs={{0,1},{1,0},{2,3},{3,2},{4,5},{5,4},{6,7},{7,6},{8,9},{9,8},{10,11... | collective-permute-start | bytes 38408 | tf_op jit(solution)/shard_map/ppermute | solution.py:1397
  629.4 4.0 copy-start.24
  636.2 4.5 copy-start.12
  636.2 4.6 copy-start.3
  640.8 4.3 copy-start.7
  643.7 1.1 copy-start.10
  643.7 1.3 copy-start.11
  645.0 3.0 copy-start.9
  645.8 5.5 copy-start.8
  645.8 10.4 %collective-permute-start.1 = (f32[3200]{0:T(1024)S(1)}, f32[3200]{0:T(1024)}, u32[]{:S(2)}, u32[]{:S(2)}) collective-permute-start(f32[3200]{0:T(1024)S(1)} %add.95), channel_id=1, source_target_pairs={{0,2},{1,3},{2,0},{3,1},{4,6},{5,7},{6,4},{7,5},{8,10},{9,11},{10,... | collective-permute-start | bytes 38408 | tf_op jit(solution)/shard_map/ppermute | solution.py:1397
  656.8 31.0 %collective-permute-start.2 = (f32[3200]{0:T(1024)S(1)}, f32[3200]{0:T(1024)S(1)}, u32[]{:S(2)}, u32[]{:S(2)}) collective-permute-start(f32[3200]{0:T(1024)S(1)} %add.96), channel_id=1, source_target_pairs={{0,4},{4,0},{8,12},{12,8},{16,20},{20,16},{24,28},{28,24},{1,5},{5... | collective-permute-start | bytes 38408 | tf_op jit(solution)/shard_map/ppermute | solution.py:1397
  687.9 30.5 %collective-permute-start.3 = (f32[3200]{0:T(1024)S(1)}, f32[3200]{0:T(1024)S(1)}, u32[]{:S(2)}, u32[]{:S(2)}) collective-permute-start(f32[3200]{0:T(1024)S(1)} %add.97), channel_id=1, source_target_pairs={{0,8},{4,12},{8,0},{12,4},{16,24},{20,28},{24,16},{28,20},{1,9},{5... | collective-permute-start | bytes 38408 | tf_op jit(solution)/shard_map/ppermute | solution.py:1397
  718.5 32.4 %collective-permute-start.4 = (f32[3200]{0:T(1024)S(1)}, f32[3200]{0:T(1024)S(1)}, u32[]{:S(2)}, u32[]{:S(2)}) collective-permute-start(f32[3200]{0:T(1024)S(1)} %add.98), channel_id=1, source_target_pairs={{0,16},{4,20},{8,24},{12,28},{16,0},{20,4},{24,8},{28,12},{1,17},{... | collective-permute-start | bytes 38408 | tf_op jit(solution)/shard_map/ppermute | solution.py:1397
  720.0 31.6 %copy-start.1 = (bf16[512,1,1536]{2,0,1:T(8,128)(2,1)S(1)}, bf16[512,1,1536]{2,0,1:T(8,128)(2,1)}, u32[]{:S(2)}) copy-start(bf16[512,1,1536]{2,0,1:T(8,128)(2,1)} %param.16) | copy-start | bytes 4718596
  742.4 6.9 copy-start.14
  742.4 7.7 %copy-start.13 = (f32[192,192]{1,0:T(8,128)S(1)}, f32[192,192]{1,0:T(8,128)}, u32[]{:S(2)}) copy-start(f32[192,192]{1,0:T(8,128)} %get-tuple-element.93) | copy-start | bytes 442372
  742.4 8.5 %copy-start.16 = (f32[3200]{0:T(1024)S(1)}, f32[3200]{0:T(1024)}, u32[]{:S(2)}) copy-start(f32[3200]{0:T(1024)} %param.27) | copy-start | bytes 38404
  742.4 8.5 %copy-start.17 = (f32[3200]{0:T(1024)S(1)}, f32[3200]{0:T(1024)}, u32[]{:S(2)}) copy-start(f32[3200]{0:T(1024)} %param.29) | copy-start | bytes 38404
  742.4 8.5 %copy-start.18 = (f32[3200]{0:T(1024)S(1)}, f32[3200]{0:T(1024)}, u32[]{:S(2)}) copy-start(f32[3200]{0:T(1024)} %param.28) | copy-start | bytes 38404
